TPU v7x, 128 devices: a whole 4x4x4 slice. The times are simulated.
128 devices in a mesh: grp: 4 (over y), fac: 32 (over z, x, core).
Axes of the slice: x: 4, y: 4, z: 4, core: 2. Of those that a mesh axis runs over, the one named last changes fastest.
Arguments:
- image_cube: float32 [32, 6144, 256], P('fac', 'grp'), may hold values from -6 to 6
- dual: bfloat16 [8, 32, 9216, 256], P(None, None, ('grp', 'fac')), may hold values from -6 to 6
- lowpass: bfloat16 [2, 4], replicated, may hold values from -2.5 to 2.5, as said below
- thresholds: float32 [8], replicated, may hold values from 4 to 16
- facet_rows: int32 [4, 32], replicated, may hold values from 24 to 72, as said below
Outputs:
- dual_next: bfloat16 [8, 32, 9216, 256], P(None, None, ('grp', 'fac'))
- prior_term: float32 [32, 6144, 256], P('fac', 'grp')
Inputs may be any that keep to these rules, and one draw needn't show every extreme that they name: `facet_rows`: every row sums to 1536; in every row some facet has exactly 72 rows and some exactly 24. `lowpass`: row d has nonzero taps only at positions 2 - d - 1 to 2 + d.
All inputs are finite; a program needn't handle non-finite values.
Results may differ from a plain program's by a relative error of at most 0.0035.
Values sent between devices are 32-bit elements; how exact they have to be, the bound alone decides.
No kernel may reach another device: no remote copies, remote signals or barrier semaphores. Data moves between devices by JAX's collectives and lax.ppermute only.
A program may use at most 128 MiB of HBM per device.

v0:
```python
import jax
import jax.numpy as jnp
from jax import lax
from jax.sharding import PartitionSpec as P


def shifted(x, axis, by):
    devices = lax.axis_size(axis)
    pairs = [(i, i + by) for i in range(devices) if 0 <= i + by < devices]
    return lax.ppermute(x, axis, pairs)


def highpass(lowpass_row):
    tap_count = lowpass_row.shape[0]
    parity = jnp.where(jnp.arange(tap_count) % 2 == 0, 1.0, -1.0).astype(jnp.float32)
    return parity * lowpass_row[::-1]


def column_filter(source, filter_taps):
    halo_rows = filter_taps.shape[0] // 2
    length = source.shape[2]
    padded = jnp.pad(source, ((0, 0), (0, 0), (halo_rows, halo_rows)))
    summed = jnp.zeros_like(source)
    for offset in range(2 * halo_rows):
        summed = summed + filter_taps[offset] * lax.slice_in_dim(
            padded, offset, offset + length, axis=2
        )
    return summed


def column_adjoint(source, filter_taps):
    halo_rows = filter_taps.shape[0] // 2
    length = source.shape[2]
    padded = jnp.pad(source, ((0, 0), (0, 0), (halo_rows, halo_rows)))
    summed = jnp.zeros_like(source)
    for offset in range(2 * halo_rows):
        begin = 2 * halo_rows - offset
        summed = summed + filter_taps[offset] * lax.slice_in_dim(
            padded, begin, begin + length, axis=2
        )
    return summed


def row_filter(extended, filter_taps, capacity):
    summed = jnp.zeros((extended.shape[0], capacity, extended.shape[2]), jnp.float32)
    for offset in range(filter_taps.shape[0]):
        summed = summed + filter_taps[offset] * lax.slice_in_dim(
            extended, offset, offset + capacity, axis=1
        )
    return summed


def row_adjoint(scaled_wide, filter_taps, extended_rows):
    capacity = scaled_wide.shape[1]
    spare = extended_rows - capacity
    summed = jnp.zeros((scaled_wide.shape[0], extended_rows, scaled_wide.shape[2]), jnp.float32)
    for offset in range(filter_taps.shape[0]):
        summed = summed + filter_taps[offset] * jnp.pad(
            scaled_wide, ((0, 0), (offset, spare - offset), (0, 0))
        )
    return summed


def on_device(image_cube, dual, lowpass, thresholds, facet_rows):
    filters_wide = lowpass.astype(jnp.float32)
    groups = lax.axis_size("fac")
    band_index = lax.axis_index("grp")
    facet_index = lax.axis_index("fac")
    local_channels, band_rows, columns = image_cube.shape
    capacity = dual.shape[2]
    halo_rows = lowpass.shape[1] // 2
    extended_rows = capacity + 2 * halo_rows
    band_lengths = lax.dynamic_index_in_dim(facet_rows, band_index, 0, keepdims=False)
    band_starts = jnp.cumsum(band_lengths) - band_lengths
    own_length = band_lengths[facet_index]
    positions = jnp.arange(capacity)
    row_index = band_starts[:, None] + positions[None, :]
    keep_mask = positions[None, :] < band_lengths[:, None]
    picked = jnp.take(image_cube, jnp.clip(row_index, 0, band_rows - 1), axis=1)
    picked = jnp.where(keep_mask[None, :, :, None], picked, 0.0)
    received = lax.all_to_all(picked, "fac", split_axis=1, concat_axis=0, tiled=True)
    own_rows = received.reshape(-1, capacity, columns)
    last_rows = lax.dynamic_slice_in_dim(own_rows, own_length - halo_rows, halo_rows, 1)
    upper_rim = shifted(last_rows, ("grp", "fac"), 1)
    lower_rim = shifted(own_rows[:, :halo_rows], ("grp", "fac"), -1)
    extended = jnp.concatenate([upper_rim, own_rows, jnp.zeros_like(upper_rim)], axis=1)
    extended = lax.dynamic_update_slice_in_dim(extended, lower_rim, halo_rows + own_length, 1)
    channels = extended.shape[0]
    valid_rows = (positions < own_length).astype(jnp.float32)[None, :, None]
    merged = jnp.zeros((channels, extended_rows, columns), jnp.float32)
    updated = []
    for dict_index in range(lowpass.shape[0]):
        low_taps = filters_wide[dict_index]
        filter_pair = (low_taps, highpass(low_taps))
        filtered = [column_filter(extended, taps_one) for taps_one in filter_pair]
        row_sums = [
            jnp.zeros((channels, extended_rows, columns), jnp.float32),
            jnp.zeros((channels, extended_rows, columns), jnp.float32),
        ]
        for row_kind in range(2):
            for column_kind in range(2):
                subband = 4 * dict_index + 2 * row_kind + column_kind
                coefficient = row_filter(filtered[column_kind], filter_pair[row_kind], capacity)
                combined = (dual[subband].astype(jnp.float32) + coefficient) * valid_rows
                magnitude = jnp.sqrt(jnp.sum(combined * combined, axis=0))
                radius = thresholds[subband]
                scaled = (combined * (radius / jnp.maximum(magnitude, radius))).astype(jnp.bfloat16)
                updated.append(scaled)
                row_sums[column_kind] = row_sums[column_kind] + row_adjoint(
                    scaled.astype(jnp.float32), filter_pair[row_kind], extended_rows
                )
        for column_kind in range(2):
            merged = merged + column_adjoint(row_sums[column_kind], filter_pair[column_kind])
    own_part = merged[:, halo_rows : halo_rows + capacity] * valid_rows
    spill_down = lax.dynamic_slice_in_dim(merged, halo_rows + own_length, halo_rows, 1)
    from_previous = shifted(spill_down, ("grp", "fac"), 1)
    from_next = shifted(merged[:, :halo_rows], ("grp", "fac"), -1)
    own_part = own_part.at[:, :halo_rows].add(from_previous)
    closing = lax.dynamic_slice_in_dim(own_part, own_length - halo_rows, halo_rows, 1) + from_next
    own_part = lax.dynamic_update_slice_in_dim(own_part, closing, own_length - halo_rows, 1)
    returned = lax.all_to_all(own_part[:, None], "fac", split_axis=0, concat_axis=1, tiled=True)
    band_positions = jnp.arange(band_rows)
    owner_facet = (
        jnp.sum((band_starts[None, :] <= band_positions[:, None]).astype(jnp.int32), axis=1) - 1
    )
    slot_index = owner_facet * capacity + band_positions - band_starts[owner_facet]
    prior_term = jnp.take(
        returned.reshape(local_channels, groups * capacity, columns), slot_index, axis=1
    )
    return (jnp.stack(updated, 0), prior_term)


def solution(mesh):
    placed = (P("fac", "grp", None), P(None, None, ("grp", "fac"), None), P(), P(), P())
    return jax.shard_map(
        on_device,
        mesh=mesh,
        in_specs=placed,
        out_specs=(P(None, None, ("grp", "fac"), None), P("fac", "grp", None)),
        check_vma=False,
    )
```

profile of v0, /device:TPU:24, one launch (start us, length us, event | category | flops | bytes accessed | tf_op | source)
XLA Modules:
  0.0 261.7 jit_solution(14113367375421093569)
XLA Ops:
  3.4 6.5 %gather_fusion = f32[2304,256]{1,0:T(8,128)} fusion(f32[1536,256]{1,0:T(8,128)S(1)} %bitcast.136, s32[3072]{0:T(1024)S(1)} %pad_clamp_fusion), kind=kCustom, calls=%fused_computation | custom fusion | bytes 4727808 | tf_op jit(solution)/shard_map/jit(_take)/gather | solution.py:79
  9.9 4.3 %select_select_fusion = f32[1,32,72,256]{3,2,0,1:T(8,128)} fusion(f32[1,32,72,256]{3,2,0,1:T(8,128)} %bitcast.141, pred[32,72]{1,0:T(8,128)(4,1)S(1)} %get-tuple-element.135, pred[32,72]{1,0:T(8,128)(4,1)S(1)} %get-tuple-element.134), kind=kLoop, calls=%fused_computation.86 | loop fusion | flops 1179648 | bytes 4723200 | tf_op jit(solution)/shard_map/jit(_where)/select_n | solution.py:80
  14.1 8.3 %all-to-all-start = ((f32[1,32,72,256]{3,2,0,1:T(8,128)}), f32[1,32,72,256]{3,2,0,1:T(8,128)S(1)}, u32[]{:S(2)}, u32[]{:S(2)}) async-start(f32[1,32,72,256]{3,2,0,1:T(8,128)} %select_select_fusion), calls=%async_computation | async-start | bytes 4718592 | tf_op jit(solution)/shard_map/all_to_all | solution.py:81
  26.8 4.4 %fusion.47 = (s32[1536]{0:T(1024)S(1)}, s32[1536,1]{0,1:T(1,128)S(1)}) fusion(s32[]{:T(128)} %bitcast.76, s32[]{:T(128)} %bitcast.77, s32[]{:T(128)} %bitcast.78, s32[]{:T(128)} %bitcast.79, s32[]{:T(128)} %bitcast.80, s32[]{:T(128)} %bitcast.82, s32[]{:T(128)} %bitcast.81, s32[1536]{0:T(1024)S(1)} %get-tuple-element.73, s32[1536]{0:T(1024)S(1)} %get-tuple-element.72), kind=kLoop, calls=%fused_computation.162 | loop fusion | flops 21504 | bytes 24604 | tf_op jit(solution)/shard_map/gather | solution.py:126
  32.4 15.6 %compare_and_fusion = (pred[1536]{0:T(1024)(128)(4,1)S(1)}, s32[1536]{0:T(1024)S(1)}) fusion(s32[1536]{0:T(1024)S(1)} %convert_reduce_fusion, pred[1536]{0:T(1024)(128)(4,1)S(1)} %get-tuple-element.38, pred[1536]{0:T(1024)(128)(4,1)S(1)} %get-tuple-element.37, pred[1536]{0:T(1024)(128)(4,1)S(1)} %get-tuple-element.36, ...), kind=kLoop, calls=%fused_computation.161 | loop fusion | flops 53760 | bytes 58468 | tf_op jit(solution)/shard_map/jit(_take)/and | solution.py:127
  50.7 4.8 %all-to-all-done = f32[1,32,72,256]{3,2,0,1:T(8,128)S(1)} async-done(((f32[1,32,72,256]{3,2,0,1:T(8,128)}), f32[1,32,72,256]{3,2,0,1:T(8,128)S(1)}, u32[]{:S(2)}, u32[]{:S(2)}) %all-to-all-start) | async-done | bytes 2359328 | tf_op jit(solution)/shard_map/all_to_all | solution.py:81
  58.2 8.0 %collective-permute-start.1 = (f32[32,2,256]{2,1,0:T(2,128)S(1)}, f32[32,2,256]{2,1,0:T(2,128)S(1)}, u32[]{:S(2)}, u32[]{:S(2)}) collective-permute-start(f32[32,2,256]{2,1,0:T(2,128)S(1)} %slice.463), channel_id=1, source_target_pairs={{1,0},{2,1},{3,2},{4,3},{5,4},{6,5},{7,6},{8,7},{9,8},{10,9},{11,1... | collective-permute-start | bytes 196616 | tf_op jit(solution)/shard_map/ppermute | solution.py:10
  68.8 4.5 %multiply_add_fusion.3 = f32[32,76,256]{2,1,0:T(8,128)S(1)} fusion(f32[32,76,256]{2,1,0:T(8,128)S(1)} %dynamic_update_slice.7, f32[]{:T(128)} %bitcast.12, f32[]{:T(128)} %bitcast.11, f32[]{:T(128)} %bitcast.10, f32[]{:T(128)} %bitcast.1), kind=kLoop, calls=%fused_computation.52 | loop fusion | flops 4358144 | bytes 4980752 | tf_op jit(solution)/shard_map/add | solution.py:25
  73.2 9.8 %multiply_reduce_fusion.5 = (f32[72,256]{1,0:T(8,128)S(1)}, f32[32,72,256]{2,1,0:T(8,128)}, f32[72,256]{1,0:T(8,128)S(1)}, f32[32,72,256]{2,1,0:T(8,128)}) fusion(f32[72]{0:T(128)S(1)} %compare_convert_fusion, f32[32,76,256]{2,1,0:T(8,128)S(1)} %multiply_add_fusion.3, f32[]{:T(128)} %bitcast.20, f32[]{:T(128)} %bitcast.19, f32[]{:T(128)} %bitcast.18, ...), kind=kLoop, calls=%fused_computation.81 | loop fusion | flops 14118912 | bytes 16662848 | tf_op jit(solution)/shard_map/reduce_sum | solution.py:105
  83.0 13.5 %multiply_add_fusion = (f32[32,76,256]{2,1,0:T(8,128)S(1)}, f32[32,76,256]{2,1,0:T(8,128)S(1)}, f32[32,76,256]{2,1,0:T(8,128)S(1)}) fusion(f32[32,76,256]{2,1,0:T(8,128)S(1)} %dynamic_update_slice.7, f32[]{:T(128)} %bitcast.41, f32[]{:T(128)} %bitcast.40, f32[]{:T(128)} %bitcast.39, f32[]{:T(128)} %bitcast.38, f32[]{:T(128)} %bitcast.33, f32[]{:T(128)} %bitcast.32, ...), kind=kLoop, calls=%fused_computation.49 | loop fusion | flops 13074432 | bytes 9961520 | tf_op jit(solution)/shard_map/add | solution.py:25
  96.6 8.5 %multiply_reduce_fusion = (f32[72,256]{1,0:T(8,128)S(1)}, f32[32,72,256]{2,1,0:T(8,128)S(1)}, f32[72,256]{1,0:T(8,128)S(1)}, f32[32,72,256]{2,1,0:T(8,128)S(1)}) fusion(f32[72]{0:T(128)S(1)} %compare_convert_fusion, f32[32,76,256]{2,1,0:T(8,128)S(1)} %get-tuple-element.69, f32[]{:T(128)} %bitcast.41, f32[]{:T(128)} %bitcast.40, f32[]{:T(128)} %bitcast.39, ...), kind=kLoop, calls=%fused_computation.71 | loop fusion | flops 14118912 | bytes 16662848 | tf_op jit(solution)/shard_map/reduce_sum | solution.py:105
  105.1 8.5 %multiply_reduce_fusion.1 = (f32[72,256]{1,0:T(8,128)S(1)}, f32[32,72,256]{2,1,0:T(8,128)S(1)}, f32[72,256]{1,0:T(8,128)S(1)}, f32[32,72,256]{2,1,0:T(8,128)S(1)}) fusion(f32[72]{0:T(128)S(1)} %compare_convert_fusion, f32[32,76,256]{2,1,0:T(8,128)S(1)} %get-tuple-element.70, f32[]{:T(128)} %bitcast.41, f32[]{:T(128)} %bitcast.40, f32[]{:T(128)} %bitcast.39, ...), kind=kLoop, calls=%fused_computation.73 | loop fusion | flops 14118912 | bytes 16662848 | tf_op jit(solution)/shard_map/reduce_sum | solution.py:105
  113.7 10.1 %multiply_reduce_fusion.4 = (f32[72,256]{1,0:T(8,128)S(1)}, f32[32,72,256]{2,1,0:T(8,128)S(1)}, f32[72,256]{1,0:T(8,128)S(1)}, f32[32,72,256]{2,1,0:T(8,128)S(1)}) fusion(f32[72]{0:T(128)S(1)} %compare_convert_fusion, f32[32,76,256]{2,1,0:T(8,128)S(1)} %get-tuple-element.71, f32[]{:T(128)} %bitcast.20, f32[]{:T(128)} %bitcast.19, f32[]{:T(128)} %bitcast.18, ...), kind=kLoop, calls=%fused_computation.79 | loop fusion | flops 14118912 | bytes 16662848 | tf_op jit(solution)/shard_map/reduce_sum | solution.py:105
  124.6 2.2 maximum_divide_fusion.7
  127.3 8.4 %add_add_fusion.3 = f32[32,76,256]{2,1,0:T(8,128)} fusion(f32[32,72,256]{2,1,0:T(8,128)S(1)} %fusion.37, f32[32,72,256]{2,1,0:T(8,128)S(1)} %fusion.35, f32[]{:T(128)} %bitcast.20, f32[]{:T(128)} %bitcast.19, f32[]{:T(128)} %bitcast.18, f32[]{:T(128)} %bitcast.17, f32[]{:T(128)} %bitcast.12, f32[]{:T(128)} %bitcast.11, f32[]{:T(128)} %bitcast.10, f32[]{:T(128)} %bitcast.1), kind=kLoop, calls=%fused_computation.48 | loop fusion | flops 9338880 | bytes 7208992 | tf_op jit(solution)/shard_map/add | solution.py:109
  137.4 8.4 %add_add_fusion = f32[32,76,256]{2,1,0:T(8,128)} fusion(f32[32,72,256]{2,1,0:T(8,128)S(1)} %fusion.42, f32[32,72,256]{2,1,0:T(8,128)S(1)} %fusion.40, f32[]{:T(128)} %bitcast.41, f32[]{:T(128)} %bitcast.40, f32[]{:T(128)} %bitcast.39, f32[]{:T(128)} %bitcast.38, f32[]{:T(128)} %bitcast.33, f32[]{:T(128)} %bitcast.32, f32[]{:T(128)} %bitcast.31, f32[]{:T(128)} %bitcast.30), kind=kLoop, calls=%fused_computation.45 | loop fusion | flops 9338880 | bytes 7208992 | tf_op jit(solution)/shard_map/add | solution.py:109
  148.8 8.2 %add_add_fusion.2 = f32[32,76,256]{2,1,0:T(8,128)} fusion(f32[32,72,256]{2,1,0:T(8,128)S(1)} %fusion.38, f32[32,72,256]{2,1,0:T(8,128)S(1)} %fusion.36, f32[]{:T(128)} %bitcast.20, f32[]{:T(128)} %bitcast.19, f32[]{:T(128)} %bitcast.18, f32[]{:T(128)} %bitcast.17, f32[]{:T(128)} %bitcast.12, f32[]{:T(128)} %bitcast.11, f32[]{:T(128)} %bitcast.10, f32[]{:T(128)} %bitcast.1), kind=kLoop, calls=%fused_computation.47 | loop fusion | flops 9338880 | bytes 7208992 | tf_op jit(solution)/shard_map/add | solution.py:109
  157.4 8.4 %add_add_fusion.1 = f32[32,76,256]{2,1,0:T(8,128)} fusion(f32[32,72,256]{2,1,0:T(8,128)S(1)} %fusion.41, f32[32,72,256]{2,1,0:T(8,128)S(1)} %fusion.39, f32[]{:T(128)} %bitcast.41, f32[]{:T(128)} %bitcast.40, f32[]{:T(128)} %bitcast.39, f32[]{:T(128)} %bitcast.38, f32[]{:T(128)} %bitcast.33, f32[]{:T(128)} %bitcast.32, f32[]{:T(128)} %bitcast.31, f32[]{:T(128)} %bitcast.30), kind=kLoop, calls=%fused_computation.46 | loop fusion | flops 9338880 | bytes 7208992 | tf_op jit(solution)/shard_map/add | solution.py:109
  165.8 34.3 %fusion.6 = f32[32,76,256]{2,1,0:T(8,128)} fusion(f32[32,76,256]{2,1,0:T(8,128)} %add_add_fusion.3, f32[32,76,256]{2,1,0:T(8,128)} %add_add_fusion.2, f32[32,76,256]{2,1,0:T(8,128)} %add_add_fusion.1, f32[32,76,256]{2,1,0:T(8,128)} %add_add_fusion, f32[]{:T(128)} %bitcast.41, f32[]{:T(128)} %bitcast.40, f32[]{:T(128)} %bitcast.39, f32[]{:T(128)} %bitcast.38, ...), kind=kLoop, calls=%fused_computation.23 | loop fusion | flops 19300352 | bytes 12451904 | tf_op jit(solution)/shard_map/add | solution.py:113
  205.2 7.9 %collective-permute-start.3 = (f32[32,2,256]{2,1,0:T(2,128)S(1)}, f32[32,2,256]{2,1,0:T(2,128)S(1)}, u32[]{:S(2)}, u32[]{:S(2)}) collective-permute-start(f32[32,2,256]{2,1,0:T(2,128)S(1)} %get-tuple-element.67), channel_id=1, source_target_pairs={{1,0},{2,1},{3,2},{4,3},{5,4},{6,5},{7,6},{8,7},{9,8},{10,9},{11,1... | collective-permute-start | bytes 196616 | tf_op jit(solution)/shard_map/ppermute | solution.py:10
  217.0 5.1 %all-to-all-start.1 = ((f32[32,1,72,256]{3,2,1,0:T(8,128)}), f32[32,1,72,256]{3,2,1,0:T(8,128)}, u32[]{:S(2)}, u32[]{:S(2)}) async-start(f32[32,1,72,256]{3,2,1,0:T(8,128)} %bitcast.138), calls=%async_computation.1 | async-start | bytes 4718592 | tf_op jit(solution)/shard_map/all_to_all | solution.py:121
  222.0 3.0 %bitcast_dynamic-update-slice_fusion.7 = bf16[8,32,72,256]{3,2,1,0:T(8,128)(2,1)} fusion(f32[32,72,256]{2,1,0:T(8,128)} %get-tuple-element.66, f32[72,256]{1,0:T(8,128)S(1)} %maximum_divide_fusion.7), kind=kLoop, calls=%fused_computation.95 | loop fusion | flops 1179647 | bytes 3612672
  238.0 16.9 %all-to-all-done.1 = f32[32,1,72,256]{3,2,1,0:T(8,128)} async-done(((f32[32,1,72,256]{3,2,1,0:T(8,128)}), f32[32,1,72,256]{3,2,1,0:T(8,128)}, u32[]{:S(2)}, u32[]{:S(2)}) %all-to-all-start.1) | async-done | bytes 2359328 | tf_op jit(solution)/shard_map/all_to_all | solution.py:121
  254.9 5.4 %gather_fusion.1 = f32[1536,256]{1,0:T(8,128)S(1)} fusion(f32[2304,256]{1,0:T(8,128)} %bitcast.86, s32[2048]{0:T(1024)S(1)} %pad_clamp_fusion.1), kind=kCustom, calls=%fused_computation.1 | custom fusion | bytes 3151872 | tf_op jit(solution)/shard_map/jit(_take)/gather | solution.py:127
  (109 shorter events, 42.9 us)
Async XLA Ops:
  0.6 2.7 %copy-start = (f32[1,1536,256]{2,1,0:T(8,128)S(1)}, f32[1,1536,256]{2,1,0:T(8,128)}, u32[]{:S(2)}) copy-start(f32[1,1536,256]{2,1,0:T(8,128)} %param.7) | copy-start | bytes 4718596
  14.1 8.3 %copy-start.19 = (s32[4,32]{1,0:T(4,128)S(1)}, s32[4,32]{1,0:T(4,128)}, u32[]{:S(2)}) copy-start(s32[4,32]{1,0:T(4,128)} %param.11) | copy-start | bytes 1540
  14.1 11.5 %copy-start.17 = (bf16[2,4]{1,0:T(2,128)(2,1)S(1)}, bf16[2,4]{1,0:T(2,128)(2,1)}, u32[]{:S(2)}) copy-start(bf16[2,4]{1,0:T(2,128)(2,1)} %param.9) | copy-start | bytes 52
  14.1 35.9 %copy-start.18 = (f32[8]{0:T(128)S(1)}, f32[8]{0:T(128)}, u32[]{:S(2)}) copy-start(f32[8]{0:T(128)} %param.10) | copy-start | bytes 100
  14.1 41.4 %all-to-all-start = ((f32[1,32,72,256]{3,2,0,1:T(8,128)}), f32[1,32,72,256]{3,2,0,1:T(8,128)S(1)}, u32[]{:S(2)}, u32[]{:S(2)}) async-start(f32[1,32,72,256]{3,2,0,1:T(8,128)} %select_select_fusion), calls=%async_computation | async-start | bytes 4718592 | tf_op jit(solution)/shard_map/all_to_all | solution.py:81
  55.5 10.7 %copy-start.16 = (f32[1,32,72,256]{3,2,0,1:T(8,128)}, f32[1,32,72,256]{3,2,0,1:T(8,128)S(1)}, u32[]{:S(2)}) copy-start(f32[1,32,72,256]{3,2,0,1:T(8,128)S(1)} %all-to-all-done) | copy-start | bytes 7077892
  55.6 10.7 %collective-permute-start = (f32[32,2,256]{2,1,0:T(2,128)S(1)}, f32[32,2,256]{2,1,0:T(2,128)S(1)}, u32[]{:S(2)}, u32[]{:S(2)}) collective-permute-start(f32[32,2,256]{2,1,0:T(2,128)S(1)} %dynamic-slice_bitcast_fusion), channel_id=1, source_target_pairs={{0,1},{1,2},{2,3},{3,4},{4,5},{5,6},{6,7},{7,8},{8,9},{9,10},{10,1... | collective-permute-start | bytes 196616 | tf_op jit(solution)/shard_map/ppermute | solution.py:10
  58.2 10.2 %collective-permute-start.1 = (f32[32,2,256]{2,1,0:T(2,128)S(1)}, f32[32,2,256]{2,1,0:T(2,128)S(1)}, u32[]{:S(2)}, u32[]{:S(2)}) collective-permute-start(f32[32,2,256]{2,1,0:T(2,128)S(1)} %slice.463), channel_id=1, source_target_pairs={{1,0},{2,1},{3,2},{4,3},{5,4},{6,5},{7,6},{8,7},{9,8},{10,9},{11,1... | collective-permute-start | bytes 196616 | tf_op jit(solution)/shard_map/ppermute | solution.py:10
  105.1 32.0 %copy-start.4 = (f32[32,72,256]{2,1,0:T(8,128)}, f32[32,72,256]{2,1,0:T(8,128)S(1)}, u32[]{:S(2)}) copy-start(f32[32,72,256]{2,1,0:T(8,128)S(1)} %get-tuple-element.60) | copy-start | bytes 7077892
  113.6 43.4 %copy-start.9 = (f32[32,72,256]{2,1,0:T(8,128)}, f32[32,72,256]{2,1,0:T(8,128)S(1)}, u32[]{:S(2)}) copy-start(f32[32,72,256]{2,1,0:T(8,128)S(1)} %get-tuple-element.62) | copy-start | bytes 7077892
  113.7 43.6 %copy-start.6 = (f32[32,72,256]{2,1,0:T(8,128)}, f32[32,72,256]{2,1,0:T(8,128)S(1)}, u32[]{:S(2)}) copy-start(f32[32,72,256]{2,1,0:T(8,128)S(1)} %get-tuple-element.46) | copy-start | bytes 7077892
  113.7 13.2 %copy-start.8 = (f32[32,72,256]{2,1,0:T(8,128)S(1)}, f32[32,72,256]{2,1,0:T(8,128)}, u32[]{:S(2)}) copy-start(f32[32,72,256]{2,1,0:T(8,128)} %get-tuple-element.66) | copy-start | bytes 7077892
  123.8 24.7 %copy-start.13 = (f32[32,72,256]{2,1,0:T(8,128)}, f32[32,72,256]{2,1,0:T(8,128)S(1)}, u32[]{:S(2)}) copy-start(f32[32,72,256]{2,1,0:T(8,128)S(1)} %get-tuple-element.64) | copy-start | bytes 7077892
  123.8 24.9 %copy-start.11 = (f32[32,72,256]{2,1,0:T(8,128)}, f32[32,72,256]{2,1,0:T(8,128)S(1)}, u32[]{:S(2)}) copy-start(f32[32,72,256]{2,1,0:T(8,128)S(1)} %get-tuple-element.52) | copy-start | bytes 7077892
  123.8 3.4 %copy-start.2 = (f32[32,72,256]{2,1,0:T(8,128)S(1)}, f32[32,72,256]{2,1,0:T(8,128)}, u32[]{:S(2)}) copy-start(f32[32,72,256]{2,1,0:T(8,128)} %get-tuple-element.54) | copy-start | bytes 7077892
  201.2 11.9 %collective-permute-start.2 = (f32[32,2,256]{2,1,0:T(2,128)S(1)}, f32[32,2,256]{2,1,0:T(2,128)S(1)}, u32[]{:S(2)}, u32[]{:S(2)}) collective-permute-start(f32[32,2,256]{2,1,0:T(2,128)S(1)} %get-tuple-element.68), channel_id=1, source_target_pairs={{0,1},{1,2},{2,3},{3,4},{4,5},{5,6},{6,7},{7,8},{8,9},{9,10},{10,1... | collective-permute-start | bytes 196616 | tf_op jit(solution)/shard_map/ppermute | solution.py:10
  205.2 9.8 %collective-permute-start.3 = (f32[32,2,256]{2,1,0:T(2,128)S(1)}, f32[32,2,256]{2,1,0:T(2,128)S(1)}, u32[]{:S(2)}, u32[]{:S(2)}) collective-permute-start(f32[32,2,256]{2,1,0:T(2,128)S(1)} %get-tuple-element.67), channel_id=1, source_target_pairs={{1,0},{2,1},{3,2},{4,3},{5,4},{6,5},{7,6},{8,7},{9,8},{10,9},{11,1... | collective-permute-start | bytes 196616 | tf_op jit(solution)/shard_map/ppermute | solution.py:10
  217.0 37.9 %all-to-all-start.1 = ((f32[32,1,72,256]{3,2,1,0:T(8,128)}), f32[32,1,72,256]{3,2,1,0:T(8,128)}, u32[]{:S(2)}, u32[]{:S(2)}) async-start(f32[32,1,72,256]{3,2,1,0:T(8,128)} %bitcast.138), calls=%async_computation.1 | async-start | bytes 4718592 | tf_op jit(solution)/shard_map/all_to_all | solution.py:121
  222.0 3.0 %copy-start.14 = (f32[32,72,256]{2,1,0:T(8,128)S(1)}, f32[32,72,256]{2,1,0:T(8,128)}, u32[]{:S(2)}) copy-start(f32[32,72,256]{2,1,0:T(8,128)} %copy-done.13) | copy-start | bytes 7077892
  225.1 2.1 copy-start.3
  227.2 2.1 copy-start.12
  229.3 2.1 copy-start.10
  231.3 2.1 copy-start.5
  254.9 6.9 %copy-start.1 = (f32[1,1536,256]{2,1,0:T(8,128)S(1)}, f32[1,1536,256]{2,1,0:T(8,128)}, u32[]{:S(2)}) copy-start(f32[1,1536,256]{2,1,0:T(8,128)} %param.7) | copy-start | bytes 4718596
  (2 other events, 3.9 us)
where the time goes:
time: 267 us; the launch traced here: 262 us
  other arithmetic  175 us (66%)
  starting transfers between devices  33.1 us (12%)
  local copies, waits for them, and re-layouts  26.5 us (10%)
  waiting for transfers between devices  23.5 us (9%)
  between operations  3.81 us (1%)
    reduce_sum x4, other arithmetic, on_device(): magnitude = jnp.sqrt(jnp.sum(combined * combined, axis=0))  36.9 us
    add x1, other arithmetic, on_device(): merged + column_adjoint(row_sums[column_kind], filter_pair[column_kind])  34.3 us
    add x4, other arithmetic, on_device(): row_sums[column_kind]  33.4 us
    ppermute x4, starting transfers between devices, shifted(): return lax.ppermute(x, axis, pairs)  19.7 us
    add x2, other arithmetic, column_filter(): summed + filter_taps[offset] * lax.slice_in_dim(padded, offset, offset +...  18 us
    all_to_all x1, waiting for transfers between devices, on_device(): lax.all_to_all(own_part[:, None], 'fac', split_axis=0, concat_axis=1, til...  16.9 us
    and x1, other arithmetic, on_device(): jnp.take(returned.reshape(local_channels, groups * capacity, columns), sl...  15.6 us
    unnamed x7, other arithmetic  10.4 us
  transfers between devices with their start and end apart: 6, of which 3 were waited for; matrix products, arithmetic and copies ran while one was open for 16% of the time, Pallas kernels for 0%

commit v1 on v0

v1 whole, which is shorter than its diff:
```python
import functools

import jax
import jax.numpy as jnp
from jax import lax
from jax.experimental import pallas as pl
from jax.experimental.pallas import tpu as pltpu
from jax.sharding import PartitionSpec as P

TAPS = 4
ABOVE = 2
MARGIN = 8
LANES = 128


def shifted(x, axis, by):
    devices = lax.axis_size(axis)
    pairs = [(i, i + by) for i in range(devices) if 0 <= i + by < devices]
    return lax.ppermute(x, axis, pairs)


def filter_taps(lowpass):
    low = lowpass.astype(jnp.float32)
    parity = jnp.where(jnp.arange(TAPS) % 2 == 0, 1.0, -1.0).astype(jnp.float32)
    return jnp.stack([low, parity * low[:, ::-1]], axis=1)


def column_matrices(taps, columns):
    row = jnp.arange(columns)[:, None]
    col = jnp.arange(columns)[None, :]
    offset = row - col + 2
    total = 0.0
    for k in range(TAPS):
        hit = (offset == k)[None, None]
        total = total + jnp.where(hit, taps[:, :, k, None, None], 0.0)
    return total.astype(jnp.bfloat16)


def facet_starts(rows_ref, starts_ref, facets):
    def step(q, total):
        starts_ref[q] = total
        return total + rows_ref[q]

    lax.fori_loop(0, facets, step, jnp.int32(0))


def pack_kernel(per_step, ext, rows_ref, image_ref, upper_ref, lower_ref, out_ref, strip, starts, sem):
    step = pl.program_id(0)
    band_rows = image_ref.shape[1]
    facets = rows_ref.shape[0]

    @pl.when(step == 0)
    def _():
        copies = [
            pltpu.make_async_copy(
                image_ref.at[0, :, pl.ds(h * LANES, LANES)],
                strip.at[h, pl.ds(MARGIN, band_rows)],
                sem.at[h],
            )
            for h in range(2)
        ]
        for copy in copies:
            copy.start()
        facet_starts(rows_ref, starts, facets)
        for h in range(2):
            lanes = slice(h * LANES, (h + 1) * LANES)
            strip[h, 0:MARGIN] = jnp.zeros((MARGIN, LANES), jnp.float32)
            strip[h, MARGIN - ABOVE : MARGIN] = upper_ref[0, :, lanes]
            tail = strip.shape[1] - MARGIN - band_rows
            strip[h, MARGIN + band_rows :] = jnp.zeros((tail, LANES), jnp.float32)
            strip[h, MARGIN + band_rows : MARGIN + band_rows + ABOVE] = lower_ref[0, :, lanes]
        for copy in copies:
            copy.wait()

    for q in range(per_step):
        begin = starts[step * per_step + q] + (MARGIN - ABOVE)
        for h in range(2):
            out_ref[q, h * ext : (h + 1) * ext] = strip[h, pl.ds(begin, ext)]


def unpack_kernel(per_step, ext, rows_ref, block_ref, from_next_ref, from_prev_ref, out_ref, strip, starts, sem):
    step = pl.program_id(0)
    band_rows = out_ref.shape[1]
    facets = rows_ref.shape[0]

    @pl.when(step == 0)
    def _():
        facet_starts(rows_ref, starts, facets)
        for h in range(2):
            strip[h, 0 : 2 * MARGIN] = jnp.zeros((2 * MARGIN, LANES), jnp.float32)

    shared = lax.broadcasted_iota(jnp.int32, (8, LANES), 0) < 3
    for q in range(per_step):
        begin = starts[step * per_step + q] + (MARGIN - ABOVE)
        for h in range(2):
            before = strip[h, pl.ds(begin, 8)]
            strip[h, pl.ds(begin, 8)] = block_ref[q, h * ext : h * ext + 8] + jnp.where(shared, before, 0.0)
            strip[h, pl.ds(begin + 8, ext - 8)] = block_ref[q, h * ext + 8 : (h + 1) * ext]

    @pl.when(step == pl.num_programs(0) - 1)
    def _():
        copies = []
        for h in range(2):
            strip[h, MARGIN : MARGIN + 1] += from_prev_ref[h]
            end = MARGIN + band_rows
            strip[h, end - ABOVE : end] += from_next_ref[h]
            copies.append(
                pltpu.make_async_copy(
                    strip.at[h, pl.ds(MARGIN, band_rows)],
                    out_ref.at[0, :, pl.ds(h * LANES, LANES)],
                    sem.at[h],
                )
            )
        for copy in copies:
            copy.start()
        for copy in copies:
            copy.wait()


def facet_kernel(group, ext, taps_ref, thr_ref, len_ref, x_ref, dual_ref, fwd_ref, adj_ref,
                 next_ref, merged_ref, u_ref, sq_ref, z_ref):
    step = pl.program_id(0)
    channels, capacity, columns = dual_ref.shape[1:]
    dict_index = step // 2
    taps = [taps_ref[step * TAPS + k] for k in range(TAPS)]
    rows = group * capacity

    @pl.when(step == 0)
    def _():
        merged_ref[...] = jnp.zeros_like(merged_ref)
        z_ref[...] = jnp.zeros_like(z_ref)

    sq_ref[...] = jnp.zeros_like(sq_ref)

    def analyse(i, carry):
        pick = pl.ds(i * group, group)
        halves = []
        for h in range(2):
            total = taps[0] * x_ref[pick, h * ext : h * ext + capacity, :]
            for k in range(1, TAPS):
                total = total + taps[k] * x_ref[pick, h * ext + k : h * ext + k + capacity, :]
            halves.append(total.reshape(rows, LANES))
        filtered = jnp.concatenate(halves, axis=1)
        high = filtered.astype(jnp.bfloat16)
        low = (filtered - high.astype(jnp.float32)).astype(jnp.bfloat16)
        coefficient = jnp.dot(
            jnp.concatenate([high, low], axis=1), fwd_ref[dict_index], preferred_element_type=jnp.float32
        )
        for b in range(2):
            part = coefficient[:, b * columns : (b + 1) * columns].reshape(group, capacity, columns)
            combined = part + dual_ref[b, pick].astype(jnp.float32)
            u_ref[b, pick] = combined
            sq_ref[b] += jnp.sum(combined * combined, axis=0)
        return carry

    lax.fori_loop(0, channels // group, analyse, 0)

    keep = lax.broadcasted_iota(jnp.int32, (capacity, columns), 0) < len_ref[0]
    for b in range(2):
        radius = thr_ref[step * 2 + b]
        scale = radius / jnp.maximum(jnp.sqrt(sq_ref[b]), radius)
        sq_ref[b] = jnp.where(keep, scale, 0.0)

    def synthesise(i, carry):
        pick = pl.ds(i * group, group)
        parts = []
        for b in range(2):
            scaled = u_ref[b, pick] * sq_ref[b][None]
            next_ref[b, pick] = scaled.astype(jnp.bfloat16)
            parts.append(scaled.reshape(rows, columns).astype(jnp.bfloat16))
        z = jnp.dot(jnp.concatenate(parts, axis=1), adj_ref[dict_index], preferred_element_type=jnp.float32)
        z = z.reshape(group, capacity, columns)
        for h in range(2):
            z_ref[h, :, 8 : 8 + capacity, :] = z[:, :, h * LANES : (h + 1) * LANES]
        for h in range(2):
            total = taps[0] * z_ref[h, :, 8 : 8 + ext, :]
            for k in range(1, TAPS):
                total = total + taps[k] * z_ref[h, :, 8 - k : 8 - k + ext, :]
            merged_ref[pick, h * ext : (h + 1) * ext, :] += total
        return carry

    lax.fori_loop(0, channels // group, synthesise, 0)


def on_device(image_cube, dual, lowpass, thresholds, facet_rows):
    band = lax.axis_index("grp")
    facet = lax.axis_index("fac")
    facets = lax.axis_size("fac")
    _, band_rows, columns = image_cube.shape
    subbands, channels, capacity, _ = dual.shape
    ext = capacity + TAPS
    per_step = 8
    strip_rows = MARGIN + band_rows + capacity
    lengths = lax.dynamic_index_in_dim(facet_rows, band, 0, keepdims=False)
    own_length = lax.dynamic_slice_in_dim(lengths, facet, 1)

    upper = shifted(image_cube[:, -ABOVE:], "grp", 1)
    lower = shifted(image_cube[:, :ABOVE], "grp", -1)
    row_scratch = [
        pltpu.VMEM((2, strip_rows, LANES), jnp.float32),
        pltpu.SMEM((facets,), jnp.int32),
        pltpu.SemaphoreType.DMA((2,)),
    ]
    blocks = pl.BlockSpec((per_step, 2 * ext, LANES), lambda i, *_: (i, 0, 0))
    smem = pl.BlockSpec(memory_space=pltpu.SMEM)
    vmem = pl.BlockSpec(memory_space=pltpu.VMEM)
    hbm = pl.BlockSpec(memory_space=pl.ANY)
    packed = pl.pallas_call(
        functools.partial(pack_kernel, per_step, ext),
        grid=(facets // per_step,),
        out_shape=jax.ShapeDtypeStruct((facets, 2 * ext, LANES), jnp.float32),
        in_specs=[smem, hbm, vmem, vmem],
        out_specs=blocks,
        scratch_shapes=row_scratch,
        compiler_params=pltpu.CompilerParams(vmem_limit_bytes=16 << 20),
        name="pack_facets",
    )(lengths, image_cube, upper, lower)

    received = lax.all_to_all(packed, "fac", split_axis=0, concat_axis=0, tiled=True)

    taps = filter_taps(lowpass)
    matrices = column_matrices(taps, columns)
    forward = jnp.concatenate([matrices[:, 0], matrices[:, 1]], axis=2)
    forward = jnp.concatenate([forward, forward], axis=1)
    swapped = jnp.swapaxes(matrices, 2, 3)
    adjoint = jnp.concatenate([swapped[:, 0], swapped[:, 1]], axis=1)
    group = 4
    steps = subbands // 2
    pair = pl.BlockSpec((2, channels, capacity, columns), lambda i: (i, 0, 0, 0))
    whole = pl.BlockSpec((channels, 2 * ext, LANES), lambda i: (0, 0, 0))
    dual_next, merged = pl.pallas_call(
        functools.partial(facet_kernel, group, ext),
        grid=(steps,),
        out_shape=(
            jax.ShapeDtypeStruct(dual.shape, jnp.bfloat16),
            jax.ShapeDtypeStruct((channels, 2 * ext, LANES), jnp.float32),
        ),
        in_specs=[
            smem, smem, smem, whole, pair,
            pl.BlockSpec(forward.shape, lambda i: (0, 0, 0)),
            pl.BlockSpec(adjoint.shape, lambda i: (0, 0, 0)),
        ],
        out_specs=(pair, whole),
        scratch_shapes=[
            pltpu.VMEM((2, channels, capacity, columns), jnp.float32),
            pltpu.VMEM((2, capacity, columns), jnp.float32),
            pltpu.VMEM((2, group, capacity + 16, LANES), jnp.float32),
        ],
        compiler_params=pltpu.CompilerParams(vmem_limit_bytes=48 << 20),
        name="facet_update",
    )(taps.reshape(-1), thresholds, own_length, received, dual, forward, adjoint)

    returned = lax.all_to_all(merged, "fac", split_axis=0, concat_axis=0, tiled=True)

    first = jnp.stack([returned[0, h * ext : h * ext + ABOVE] for h in range(2)])
    below = capacity * 0 + lengths[facets - 1] + ABOVE
    last = jnp.stack(
        [lax.dynamic_slice_in_dim(returned[facets - 1, h * ext : (h + 1) * ext], below, 1) for h in range(2)]
    )
    from_next = shifted(first, "grp", -1)
    from_prev = shifted(last, "grp", 1)
    prior_term = pl.pallas_call(
        functools.partial(unpack_kernel, per_step, ext),
        grid=(facets // per_step,),
        out_shape=jax.ShapeDtypeStruct(image_cube.shape, jnp.float32),
        in_specs=[smem, blocks, vmem, vmem],
        out_specs=hbm,
        scratch_shapes=row_scratch,
        compiler_params=pltpu.CompilerParams(vmem_limit_bytes=16 << 20),
        name="unpack_facets",
    )(lengths, returned, from_next, from_prev)
    return dual_next, prior_term


def solution(mesh):
    placed = (P("fac", "grp", None), P(None, None, ("grp", "fac"), None), P(), P(), P())
    return jax.shard_map(
        on_device,
        mesh=mesh,
        in_specs=placed,
        out_specs=(P(None, None, ("grp", "fac"), None), P("fac", "grp", None)),
        check_vma=False,
    )
```

time: 267 us -> 133 us (0.50); the launches traced: 262 us -> 132 us
  other arithmetic: 175 us -> 1.26 us
  waiting for transfers between devices: 23.5 us -> 72.3 us
  Pallas kernels: 0 us -> 30.4 us
  local copies, waits for them, and re-layouts: 26.5 us -> 6.2 us
  starting transfers between devices: 33.1 us -> 19.9 us
    add x7 -> x0, other arithmetic: 85.7 us -> none  [the longest x1 34.3 us: on_device(): merged + column_adjoint(row_sums[column_kind], filter_pair[column_kind])]
    all_to_all x2, waiting for transfers between devices: 21.7 us -> 64.6 us  [the longest x1 32.7 us: on_device(): lax.all_to_all(merged, 'fac', split_axis=0, concat_axis=0, tiled=True)]
    reduce_sum x5 -> x0, other arithmetic: 37 us -> none  [the longest x4 36.9 us: on_device(): magnitude = jnp.sqrt(jnp.sum(combined * combined, axis=0))]
    pallas_call x0 -> x3, Pallas kernels: none -> 30.4 us  [the longest x1 25.5 us: on_device(): pl.pallas_call(functools.partial(facet_kernel, group, ext), grid=(steps,)...]
    and x1 -> x0, other arithmetic: 15.6 us -> none  [on_device(): jnp.take(returned.reshape(local_channels, groups * capacity, columns), sl...]
    gather x4 -> x0, local copies, waits for them, and re-layouts: 13.4 us -> none  [the longest x1 6.47 us: on_device(): picked = jnp.take(image_cube, jnp.clip(row_index, 0, band_rows - 1), axis=1)]
    ppermute x4, starting transfers between devices: 19.7 us -> 7.57 us  [shifted(): return lax.ppermute(x, axis, pairs)]
    unnamed x7 -> x0, other arithmetic: 10.4 us -> none
  transfers between devices with their start and end apart: 6 -> 6, of which waited for: 3 -> 4; matrix products, arithmetic and copies ran while one was open for 16% -> 3% of each run, Pallas kernels for 0% -> 0%
where the time goes in v1:
time: 133 us; the launch traced here: 132 us
  waiting for transfers between devices  72.3 us (54%)
  Pallas kernels  30.4 us (23%)
  starting transfers between devices  19.9 us (15%)
  local copies, waits for them, and re-layouts  6.2 us (5%)
  between operations  2.17 us (2%)
    all_to_all x1, waiting for transfers between devices, on_device(): lax.all_to_all(merged, 'fac', split_axis=0, concat_axis=0, tiled=True)  32.7 us
    all_to_all x1, waiting for transfers between devices, on_device(): lax.all_to_all(packed, 'fac', split_axis=0, concat_axis=0, tiled=True)  31.9 us
    pallas_call x1, Pallas kernels, on_device(): pl.pallas_call(functools.partial(facet_kernel, group, ext), grid=(steps,)...  25.5 us
    all_to_all x1, starting transfers between devices, on_device(): lax.all_to_all(packed, 'fac', split_axis=0, concat_axis=0, tiled=True)  8.29 us
    ppermute x4, waiting for transfers between devices, shifted(): return lax.ppermute(x, axis, pairs)  7.65 us
    ppermute x4, starting transfers between devices, shifted(): return lax.ppermute(x, axis, pairs)  7.57 us
    all_to_all x1, starting transfers between devices, on_device(): lax.all_to_all(merged, 'fac', split_axis=0, concat_axis=0, tiled=True)  4.06 us
    unnamed x10, local copies, waits for them, and re-layouts  2.9 us
  transfers between devices with their start and end apart: 6, of which 4 were waited for; matrix products, arithmetic and copies ran while one was open for 3% of the time, Pallas kernels for 0%

profile of v1, /device:TPU:24, one launch (start us, length us, event | category | flops | bytes accessed | tf_op | source)
XLA Modules:
  0.0 132.2 jit_solution(7400920137114470419)
XLA Ops:
  0.6 0.7 fusion.14
  1.4 2.6 %collective-permute-start.1 = (f32[1,2,256]{2,1,0:T(2,128)S(1)}, f32[1,2,256]{2,1,0:T(2,128)S(1)}, u32[]{:S(2)}, u32[]{:S(2)}) collective-permute-start(f32[1,2,256]{2,1,0:T(2,128)S(1)} %get-tuple-element.10), channel_id=1, source_target_pairs={{32,0},{64,32},{96,64},{33,1},{65,33},{97,65},{34,2},{66,34},{98,6... | collective-permute-start | bytes 6152 | tf_op jit(solution)/shard_map/ppermute | solution.py:19
  4.0 1.3 collective-permute-start
  5.3 0.7 fusion.15.rows_ref
  6.0 3.5 %collective-permute-done.upper_ref = f32[1,2,256]{2,1,0:T(2,128)S(1)} collective-permute-done((f32[1,2,256]{2,1,0:T(2,128)S(1)}, f32[1,2,256]{2,1,0:T(2,128)S(1)}, u32[]{:S(2)}, u32[]{:S(2)}) %collective-permute-start) | collective-permute-done | bytes 2080 | tf_op jit(solution)/shard_map/ppermute | solution.py:19
  9.5 1.4 %copy-done.1 = f32[1,1536,256]{2,1,0:T(8,128)S(1)} copy-done((f32[1,1536,256]{2,1,0:T(8,128)S(1)}, f32[1,1536,256]{2,1,0:T(8,128)}, u32[]{:S(2)}) %copy-start.1) | copy-done | bytes 1572888
  10.9 2.8 %pack_facets.1 = f32[32,152,128]{2,1,0:T(8,128)} custom-call(s32[32]{0:T(128)S(1)} %fusion.15.rows_ref, f32[1,1536,256]{2,1,0:T(8,128)S(1)} %copy-done.1, f32[1,2,256]{2,1,0:T(2,128)S(1)} %collective-permute-done.upper_ref, f32[1,2,256]{2,1,0:T(2,128)S(1)} %collective-permute-done.1.lower_ref), custom_call_target="tpu_custom_call" | custom-call | tf_op jit(solution)/shard_map/pack_facets/pallas_call | solution.py:208
  13.7 8.3 %all-to-all-start = ((f32[32,152,128]{2,1,0:T(8,128)}), f32[32,152,128]{2,1,0:T(8,128)}, u32[]{:S(2)}, u32[]{:S(2)}) async-start(f32[32,152,128]{2,1,0:T(8,128)} %pack_facets.1), calls=%async_computation | async-start | bytes 4980736 | tf_op jit(solution)/shard_map/all_to_all | solution.py:219
  22.3 0.1 copy.16
  22.4 0.1 copy.17
  22.5 0.1 copy.18
  22.6 0.1 copy.19
  22.7 0.6 dynamic_slice.15
  23.7 0.7 add_convert_fusion
  24.7 31.9 %all-to-all-done.x_ref = f32[32,152,128]{2,1,0:T(8,128)} async-done(((f32[32,152,128]{2,1,0:T(8,128)}), f32[32,152,128]{2,1,0:T(8,128)}, u32[]{:S(2)}, u32[]{:S(2)}) %all-to-all-start) | async-done | bytes 2490400 | tf_op jit(solution)/shard_map/all_to_all | solution.py:219
  56.6 25.5 %facet_update.1 = (bf16[8,32,72,256]{3,2,1,0:T(8,128)(2,1)}, f32[32,152,128]{2,1,0:T(8,128)S(1)}) custom-call(f32[16]{0:T(128)S(1)} %reshape.77.taps_ref, f32[8]{0:T(128)S(1)} %copy-done.2, s32[1]{0:T(128)} %bitcast.2.len_ref, f32[32,152,128]{2,1,0:T(8,128)} %all-to-all-done.x_ref, bf16[8,32,72,256]{3,2,1,0:T(8,128)(2,1)} %dual_ref.1, ...), custom_call_target="tpu_custom_call" | custom-call | tf_op jit(solution)/shard_map/facet_update/pallas_call | solution.py:231
  82.1 1.5 %copy-done = f32[32,152,128]{2,1,0:T(8,128)} copy-done((f32[32,152,128]{2,1,0:T(8,128)}, f32[32,152,128]{2,1,0:T(8,128)S(1)}, u32[]{:S(2)}) %copy-start) | copy-done | bytes 2490392
  83.5 4.1 %all-to-all-start.1 = ((f32[32,152,128]{2,1,0:T(8,128)}), f32[32,152,128]{2,1,0:T(8,128)S(1)}, u32[]{:S(2)}, u32[]{:S(2)}) async-start(f32[32,152,128]{2,1,0:T(8,128)} %copy-done), calls=%async_computation.1 | async-start | bytes 4980736 | tf_op jit(solution)/shard_map/all_to_all | solution.py:253
  87.6 0.6 slice.59
  89.5 32.7 %all-to-all-done.1.block_ref = f32[32,152,128]{2,1,0:T(8,128)S(1)} async-done(((f32[32,152,128]{2,1,0:T(8,128)}), f32[32,152,128]{2,1,0:T(8,128)S(1)}, u32[]{:S(2)}, u32[]{:S(2)}) %all-to-all-start.1) | async-done | bytes 2490400 | tf_op jit(solution)/shard_map/all_to_all | solution.py:253
  122.2 2.4 %collective-permute-start.2 = (f32[2,2,128]{2,1,0:T(2,128)S(1)}, f32[2,2,128]{2,1,0:T(2,128)S(1)}, u32[]{:S(2)}, u32[]{:S(2)}) collective-permute-start(f32[2,2,128]{2,1,0:T(2,128)S(1)} %pad_maximum_fusion.2), channel_id=1, source_target_pairs={{32,0},{64,32},{96,64},{33,1},{65,33},{97,65},{34,2},{66,34},{98,6... | collective-permute-start | bytes 6152 | tf_op jit(solution)/shard_map/ppermute | solution.py:19
  124.6 1.3 collective-permute-start.3
  125.9 4.2 %collective-permute-done.3.from_prev_ref = f32[2,1,128]{2,1,0:T(1,128)S(1)} collective-permute-done((f32[2,1,128]{2,1,0:T(1,128)S(1)}, f32[2,1,128]{2,1,0:T(1,128)S(1)}, u32[]{:S(2)}, u32[]{:S(2)}) %collective-permute-start.3) | collective-permute-done | bytes 1056 | tf_op jit(solution)/shard_map/ppermute | solution.py:19
  130.1 2.2 %unpack_facets.1 = f32[1,1536,256]{2,1,0:T(8,128)} custom-call(s32[32]{0:T(128)S(1)} %fusion.15.rows_ref, f32[32,152,128]{2,1,0:T(8,128)S(1)} %all-to-all-done.1.block_ref, f32[2,2,128]{2,1,0:T(2,128)S(1)} %collective-permute-done.2.from_next_ref, f32[2,1,128]{2,1,0:T(1,128)S(1)} %collective-permute-done.3.from_prev_ref), custom_call_target="tpu_custom_call" | custom-call | tf_op jit(solution)/shard_map/unpack_facets/pallas_call | solution.py:262
  (36 shorter events, 0.9 us)
Async XLA Ops:
  1.4 4.6 %collective-permute-start.1 = (f32[1,2,256]{2,1,0:T(2,128)S(1)}, f32[1,2,256]{2,1,0:T(2,128)S(1)}, u32[]{:S(2)}, u32[]{:S(2)}) collective-permute-start(f32[1,2,256]{2,1,0:T(2,128)S(1)} %get-tuple-element.10), channel_id=1, source_target_pairs={{32,0},{64,32},{96,64},{33,1},{65,33},{97,65},{34,2},{66,34},{98,6... | collective-permute-start | bytes 6152 | tf_op jit(solution)/shard_map/ppermute | solution.py:19
  4.0 5.5 %collective-permute-start = (f32[1,2,256]{2,1,0:T(2,128)S(1)}, f32[1,2,256]{2,1,0:T(2,128)S(1)}, u32[]{:S(2)}, u32[]{:S(2)}) collective-permute-start(f32[1,2,256]{2,1,0:T(2,128)S(1)} %get-tuple-element.11), channel_id=1, source_target_pairs={{0,32},{32,64},{64,96},{1,33},{33,65},{65,97},{2,34},{34,66},{66,9... | collective-permute-start | bytes 6152 | tf_op jit(solution)/shard_map/ppermute | solution.py:19
  9.5 1.4 %copy-start.1 = (f32[1,1536,256]{2,1,0:T(8,128)S(1)}, f32[1,1536,256]{2,1,0:T(8,128)}, u32[]{:S(2)}) copy-start(f32[1,1536,256]{2,1,0:T(8,128)} %image_ref.1) | copy-start | bytes 4718596
  13.7 8.3 %copy-start.4 = (bf16[2,4]{1,0:T(2,128)(2,1)S(1)}, bf16[2,4]{1,0:T(2,128)(2,1)}, u32[]{:S(2)}) copy-start(bf16[2,4]{1,0:T(2,128)(2,1)} %param.7) | copy-start | bytes 52
  13.7 9.0 %copy-start.3 = (s32[4,32]{1,0:T(4,128)S(1)}, s32[4,32]{1,0:T(4,128)}, u32[]{:S(2)}) copy-start(s32[4,32]{1,0:T(4,128)} %param.9) | copy-start | bytes 1540
  13.7 42.9 %all-to-all-start = ((f32[32,152,128]{2,1,0:T(8,128)}), f32[32,152,128]{2,1,0:T(8,128)}, u32[]{:S(2)}, u32[]{:S(2)}) async-start(f32[32,152,128]{2,1,0:T(8,128)} %pack_facets.1), calls=%async_computation | async-start | bytes 4980736 | tf_op jit(solution)/shard_map/all_to_all | solution.py:219
  24.4 32.2 %copy-start.2 = (f32[8]{0:T(128)S(1)}, f32[8]{0:T(128)}, u32[]{:S(2)}) copy-start(f32[8]{0:T(128)} %thr_ref.1) | copy-start | bytes 100
  82.1 1.5 %copy-start = (f32[32,152,128]{2,1,0:T(8,128)}, f32[32,152,128]{2,1,0:T(8,128)S(1)}, u32[]{:S(2)}) copy-start(f32[32,152,128]{2,1,0:T(8,128)S(1)} %get-tuple-element.5) | copy-start | bytes 7471108
  83.5 38.6 %all-to-all-start.1 = ((f32[32,152,128]{2,1,0:T(8,128)}), f32[32,152,128]{2,1,0:T(8,128)S(1)}, u32[]{:S(2)}, u32[]{:S(2)}) async-start(f32[32,152,128]{2,1,0:T(8,128)} %copy-done), calls=%async_computation.1 | async-start | bytes 4980736 | tf_op jit(solution)/shard_map/all_to_all | solution.py:253
  122.2 7.9 %collective-permute-start.2 = (f32[2,2,128]{2,1,0:T(2,128)S(1)}, f32[2,2,128]{2,1,0:T(2,128)S(1)}, u32[]{:S(2)}, u32[]{:S(2)}) collective-permute-start(f32[2,2,128]{2,1,0:T(2,128)S(1)} %pad_maximum_fusion.2), channel_id=1, source_target_pairs={{32,0},{64,32},{96,64},{33,1},{65,33},{97,65},{34,2},{66,34},{98,6... | collective-permute-start | bytes 6152 | tf_op jit(solution)/shard_map/ppermute | solution.py:19
  124.6 5.5 %collective-permute-start.3 = (f32[2,1,128]{2,1,0:T(1,128)S(1)}, f32[2,1,128]{2,1,0:T(1,128)S(1)}, u32[]{:S(2)}, u32[]{:S(2)}) collective-permute-start(f32[2,1,128]{2,1,0:T(1,128)S(1)} %pad_maximum_fusion.3), channel_id=1, source_target_pairs={{0,32},{32,64},{64,96},{1,33},{33,65},{65,97},{2,34},{34,66},{66,9... | collective-permute-start | bytes 3080 | tf_op jit(solution)/shard_map/ppermute | solution.py:19

commit v2 on v1

v2 whole, which is shorter than its diff:
```python
import functools

import jax
import jax.numpy as jnp
from jax import lax
from jax.experimental import pallas as pl
from jax.experimental.pallas import tpu as pltpu
from jax.sharding import PartitionSpec as P

TAPS = 4
ABOVE = 2
MARGIN = 8
LANES = 128


def border_shift(x, bands, facets, by):
    pairs = []
    for b in range(bands):
        for facet in range(facets):
            to = b + by if facet < facets // 2 else b - by
            pairs.append((b * facets + facet, (to % bands) * facets + facet))
    return lax.ppermute(x, ("grp", "fac"), pairs)


def filter_taps(lowpass):
    low = lowpass.astype(jnp.float32)
    parity = jnp.where(jnp.arange(TAPS) % 2 == 0, 1.0, -1.0).astype(jnp.float32)
    return jnp.stack([low, parity * low[:, ::-1]], axis=1)


def column_matrices(taps, columns):
    row = jnp.arange(columns)[:, None]
    col = jnp.arange(columns)[None, :]
    offset = row - col + 2
    total = 0.0
    for k in range(TAPS):
        hit = (offset == k)[None, None]
        total = total + jnp.where(hit, taps[:, :, k, None, None], 0.0)
    return total.astype(jnp.bfloat16)


def facet_starts(rows_ref, starts_ref, facets):
    band = lax.axis_index("grp")

    def step(q, total):
        starts_ref[q] = total
        return total + rows_ref[band, q]

    lax.fori_loop(0, facets, step, jnp.int32(0))


def pack_kernel(per_copy, ext, rows_ref, image_ref, out_ref, strip, starts, blocks, in_sem, out_sem):
    band_rows = image_ref.shape[1]
    facets = rows_ref.shape[1]
    copies = [
        pltpu.make_async_copy(
            image_ref.at[0, :, pl.ds(h * LANES, LANES)], strip.at[h, pl.ds(MARGIN, band_rows)], in_sem.at[h]
        )
        for h in range(2)
    ]
    for copy in copies:
        copy.start()
    facet_starts(rows_ref, starts, facets)
    end = MARGIN + band_rows
    for h in range(2):
        strip[h, 0:MARGIN] = jnp.zeros((MARGIN, LANES), jnp.float32)
        strip[h, end:] = jnp.zeros((strip.shape[1] - end, LANES), jnp.float32)
    for copy in copies:
        copy.wait()
    for h in range(2):
        strip[h, MARGIN - ABOVE : MARGIN] = strip[h, end - ABOVE : end]
        strip[h, end : end + 1] = strip[h, MARGIN : MARGIN + 1]

    outs = []
    for g in range(facets // per_copy):
        for q in range(g * per_copy, (g + 1) * per_copy):
            begin = starts[q] + (MARGIN - ABOVE)
            for h in range(2):
                blocks[q, h * ext : (h + 1) * ext] = strip[h, pl.ds(begin, ext)]
        pick = pl.ds(g * per_copy, per_copy)
        outs.append(pltpu.make_async_copy(blocks.at[pick], out_ref.at[pick], out_sem.at[g]))
        outs[-1].start()
    for copy in outs:
        copy.wait()


def unpack_kernel(per_step, ext, rows_ref, block_ref, out_ref, strip, starts, sem):
    step = pl.program_id(0)
    band_rows = out_ref.shape[1]
    facets = rows_ref.shape[1]

    @pl.when(step == 0)
    def _():
        facet_starts(rows_ref, starts, facets)
        for h in range(2):
            strip[h, 0 : 2 * MARGIN] = jnp.zeros((2 * MARGIN, LANES), jnp.float32)

    shared = lax.broadcasted_iota(jnp.int32, (8, LANES), 0) < 3
    for q in range(per_step):
        begin = starts[step * per_step + q] + (MARGIN - ABOVE)
        for h in range(2):
            before = strip[h, pl.ds(begin, 8)]
            strip[h, pl.ds(begin, 8)] = block_ref[q, h * ext : h * ext + 8] + jnp.where(shared, before, 0.0)
            strip[h, pl.ds(begin + 8, ext - 8)] = block_ref[q, h * ext + 8 : (h + 1) * ext]

    @pl.when(step == pl.num_programs(0) - 1)
    def _():
        copies = []
        end = MARGIN + band_rows
        for h in range(2):
            strip[h, end - ABOVE : end] += strip[h, MARGIN - ABOVE : MARGIN]
            strip[h, MARGIN : MARGIN + 1] += strip[h, end : end + 1]
            copies.append(
                pltpu.make_async_copy(
                    strip.at[h, pl.ds(MARGIN, band_rows)],
                    out_ref.at[0, :, pl.ds(h * LANES, LANES)],
                    sem.at[h],
                )
            )
        for copy in copies:
            copy.start()
        for copy in copies:
            copy.wait()


def facet_kernel(group, ext, taps_ref, thr_ref, info_ref, edge_ref, x_hbm, dual_ref, fwd_ref, adj_ref,
                 next_ref, merged_ref, spill_ref, x_ref, u_ref, sq_ref, z_ref, in_sem):
    step = pl.program_id(0)
    channels, capacity, columns = dual_ref.shape[1:]
    dict_index = step // 2
    taps = [taps_ref[step * TAPS + k] for k in range(TAPS)]
    rows = group * capacity
    length, below, above = info_ref[0], info_ref[1], info_ref[2]
    inside = info_ref[3].astype(jnp.float32)

    def incoming(i):
        pick = pl.ds(i * group, group)
        return pltpu.make_async_copy(x_hbm.at[pick], x_ref.at[pick], in_sem.at[i])

    @pl.when(step == 0)
    def _():
        for i in range(channels // group):
            incoming(i).start()
        merged_ref[...] = jnp.zeros_like(merged_ref)
        z_ref[...] = jnp.zeros_like(z_ref)

    sq_ref[...] = jnp.zeros_like(sq_ref)

    def analyse(i, carry):
        pick = pl.ds(i * group, group)

        @pl.when(step == 0)
        def _():
            incoming(i).wait()

            @pl.when(above == 1)
            def _():
                for h in range(2):
                    x_ref[pick, h * ext : h * ext + ABOVE, :] = inside * edge_ref[pick, ABOVE * h : ABOVE * (h + 1), :]

            @pl.when(below == 1)
            def _():
                for h in range(2):
                    row = pl.ds(h * ext + ABOVE + length, 1)
                    x_ref[pick, row, :] = inside * edge_ref[pick, ABOVE * h : ABOVE * h + 1, :]

        halves = []
        for h in range(2):
            total = taps[0] * x_ref[pick, h * ext : h * ext + capacity, :]
            for k in range(1, TAPS):
                total = total + taps[k] * x_ref[pick, h * ext + k : h * ext + k + capacity, :]
            halves.append(total.reshape(rows, LANES))
        filtered = jnp.concatenate(halves, axis=1)
        high = filtered.astype(jnp.bfloat16)
        low = (filtered - high.astype(jnp.float32)).astype(jnp.bfloat16)
        coefficient = jnp.dot(
            jnp.concatenate([high, low], axis=1), fwd_ref[dict_index], preferred_element_type=jnp.float32
        )
        for b in range(2):
            part = coefficient[:, b * columns : (b + 1) * columns].reshape(group, capacity, columns)
            combined = part + dual_ref[b, pick].astype(jnp.float32)
            u_ref[b, pick] = combined
            sq_ref[b] += jnp.sum(combined * combined, axis=0)
        return carry

    lax.fori_loop(0, channels // group, analyse, 0)

    keep = lax.broadcasted_iota(jnp.int32, (capacity, columns), 0) < length
    for b in range(2):
        radius = thr_ref[step * 2 + b]
        scale = radius / jnp.maximum(jnp.sqrt(sq_ref[b]), radius)
        sq_ref[b] = jnp.where(keep, scale, 0.0)

    def synthesise(i, carry):
        pick = pl.ds(i * group, group)
        parts = []
        for b in range(2):
            scaled = u_ref[b, pick] * sq_ref[b][None]
            next_ref[b, pick] = scaled.astype(jnp.bfloat16)
            parts.append(scaled.reshape(rows, columns).astype(jnp.bfloat16))
        z = jnp.dot(jnp.concatenate(parts, axis=1), adj_ref[dict_index], preferred_element_type=jnp.float32)
        z = z.reshape(group, capacity, columns)
        for h in range(2):
            z_ref[h, :, 8 : 8 + capacity, :] = z[:, :, h * LANES : (h + 1) * LANES]
        for h in range(2):
            total = taps[0] * z_ref[h, :, 8 : 8 + ext, :]
            for k in range(1, TAPS):
                total = total + taps[k] * z_ref[h, :, 8 - k : 8 - k + ext, :]
            merged_ref[pick, h * ext : (h + 1) * ext, :] += total

        return carry

    lax.fori_loop(0, channels // group, synthesise, 0)

    @pl.when(step == pl.num_programs(0) - 1)
    def _():
        spill_ref[...] = jnp.zeros_like(spill_ref)

        @pl.when(above == 1)
        def _():
            for h in range(2):
                spill_ref[:, ABOVE * h : ABOVE * (h + 1), :] = merged_ref[:, h * ext : h * ext + ABOVE, :]

        @pl.when(below == 1)
        def _():
            for h in range(2):
                spill_ref[:, ABOVE * h : ABOVE * h + 1, :] = merged_ref[:, pl.ds(h * ext + ABOVE + length, 1), :]


def border_kernel(ext, info_ref, merged_ref, spill_ref, out_ref, sem):
    length, below, above = info_ref[0], info_ref[1], info_ref[2]
    inside = info_ref[4].astype(jnp.float32)

    @pl.when(above == 1)
    def _():
        for h in range(2):
            merged_ref[:, h * ext : h * ext + ABOVE, :] = inside * spill_ref[:, ABOVE * h : ABOVE * (h + 1), :]

    @pl.when(below == 1)
    def _():
        for h in range(2):
            row = pl.ds(h * ext + ABOVE + length, 1)
            merged_ref[:, row, :] = inside * spill_ref[:, ABOVE * h : ABOVE * h + 1, :]

    copy = pltpu.make_async_copy(merged_ref, out_ref, sem)
    copy.start()
    copy.wait()


def on_device(image_cube, dual, lowpass, thresholds, facet_rows):
    band = lax.axis_index("grp")
    facet = lax.axis_index("fac")
    facets = lax.axis_size("fac")
    bands = lax.axis_size("grp")
    _, band_rows, columns = image_cube.shape
    subbands, channels, capacity, _ = dual.shape
    ext = capacity + TAPS
    per_step = 8
    strip_rows = MARGIN + band_rows + capacity
    lengths = lax.dynamic_index_in_dim(facet_rows, band, 0, keepdims=False)
    own_length = lax.dynamic_slice_in_dim(lengths, facet, 1)

    row_scratch = [
        pltpu.VMEM((2, strip_rows, LANES), jnp.float32),
        pltpu.SMEM((facets,), jnp.int32),
        pltpu.SemaphoreType.DMA((2,)),
    ]
    blocks = pl.BlockSpec((per_step, 2 * ext, LANES), lambda i, *_: (i, 0, 0))
    smem = pl.BlockSpec(memory_space=pltpu.SMEM)
    vmem = pl.BlockSpec(memory_space=pltpu.VMEM)
    hbm = pl.BlockSpec(memory_space=pltpu.HBM)
    packed = pl.pallas_call(
        functools.partial(pack_kernel, per_step, ext),
        out_shape=pltpu.HBM((facets, 2 * ext, LANES), jnp.float32),
        in_specs=[smem, hbm],
        out_specs=hbm,
        scratch_shapes=row_scratch[:2] + [
            pltpu.VMEM((facets, 2 * ext, LANES), jnp.float32),
            pltpu.SemaphoreType.DMA((2,)),
            pltpu.SemaphoreType.DMA((facets // per_step,)),
        ],
        compiler_params=pltpu.CompilerParams(vmem_limit_bytes=16 << 20),
        name="pack_facets",
    )(facet_rows, pltpu.with_memory_space_constraint(image_cube, pltpu.HBM))

    received = lax.all_to_all(packed, "fac", split_axis=0, concat_axis=0, tiled=True)

    taps = filter_taps(lowpass)
    matrices = column_matrices(taps, columns)
    forward = jnp.concatenate([matrices[:, 0], matrices[:, 1]], axis=2)
    forward = jnp.concatenate([forward, forward], axis=1)
    swapped = jnp.swapaxes(matrices, 2, 3)
    adjoint = jnp.concatenate([swapped[:, 0], swapped[:, 1]], axis=1)
    group = 16
    steps = subbands // 2
    pair = pl.BlockSpec((2, channels, capacity, columns), lambda i: (i, 0, 0, 0))
    below = facet == facets - 1
    above = facet == 0
    before = jnp.where(above, band > 0, band < bands - 1)
    after = jnp.where(above, band < bands - 1, band > 0)
    flags = [flag.astype(jnp.int32) for flag in (below, above, before, after)]
    info = jnp.stack([own_length[0]] + flags)
    edge_row = jnp.where(above, 0, own_length[0] + ABOVE)
    edges = [lax.dynamic_slice_in_dim(received, h * ext + edge_row, ABOVE, 1) for h in range(2)]
    edges = border_shift(jnp.concatenate(edges, axis=1), bands, facets, 1)
    dual_next, merged, spill = pl.pallas_call(
        functools.partial(facet_kernel, group, ext),
        grid=(steps,),
        out_shape=(
            jax.ShapeDtypeStruct(dual.shape, jnp.bfloat16),
            jax.ShapeDtypeStruct(received.shape, jnp.float32),
            jax.ShapeDtypeStruct(edges.shape, jnp.float32),
        ),
        in_specs=[
            smem, smem, smem, vmem, hbm, pair,
            pl.BlockSpec(forward.shape, lambda i: (0, 0, 0)),
            pl.BlockSpec(adjoint.shape, lambda i: (0, 0, 0)),
        ],
        out_specs=(pair, vmem, vmem),
        scratch_shapes=[
            pltpu.VMEM((channels, 2 * ext, LANES), jnp.float32),
            pltpu.VMEM((2, channels, capacity, columns), jnp.float32),
            pltpu.VMEM((2, capacity, columns), jnp.float32),
            pltpu.VMEM((2, group, capacity + 16, LANES), jnp.float32),
            pltpu.SemaphoreType.DMA((channels // group,)),
        ],
        compiler_params=pltpu.CompilerParams(vmem_limit_bytes=44 << 20),
        name="facet_update",
    )(taps.reshape(-1), thresholds, info, edges, received, dual, forward, adjoint)

    spill = border_shift(spill, bands, facets, -1)
    merged = pl.pallas_call(
        functools.partial(border_kernel, ext),
        out_shape=pltpu.HBM(received.shape, jnp.float32),
        in_specs=[smem, vmem, vmem],
        out_specs=hbm,
        scratch_shapes=[pltpu.SemaphoreType.DMA],
        compiler_params=pltpu.CompilerParams(vmem_limit_bytes=16 << 20),
        name="add_border_rows",
    )(info, merged, spill)
    returned = lax.all_to_all(merged, "fac", split_axis=0, concat_axis=0, tiled=True)

    prior_term = pl.pallas_call(
        functools.partial(unpack_kernel, per_step, ext),
        grid=(facets // per_step,),
        out_shape=jax.ShapeDtypeStruct(image_cube.shape, jnp.float32),
        in_specs=[smem, blocks],
        out_specs=hbm,
        scratch_shapes=row_scratch,
        compiler_params=pltpu.CompilerParams(vmem_limit_bytes=16 << 20),
        name="unpack_facets",
    )(facet_rows, returned)
    return dual_next, prior_term


def solution(mesh):
    placed = (P("fac", "grp", None), P(None, None, ("grp", "fac"), None), P(), P(), P())
    return jax.shard_map(
        on_device,
        mesh=mesh,
        in_specs=placed,
        out_specs=(P(None, None, ("grp", "fac"), None), P("fac", "grp", None)),
        check_vma=False,
    )
```

time: 133 us -> 120 us (0.902)
  blocking collectives: 0 us -> 36.8 us
  waiting for transfers between devices: 72.3 us -> 37.5 us
  starting transfers between devices: 19.9 us -> 9.28 us
  Pallas kernels: 30.4 us -> 27.2 us
  local copies, waits for them, and re-layouts: 6.2 us -> 3.5 us
    all_to_all x0 -> x1, blocking collectives: none -> 36.8 us  [on_device(): lax.all_to_all(merged, 'fac', split_axis=0, concat_axis=0, tiled=True)]
    all_to_all x1 -> x0, waiting for transfers between devices: 32.7 us -> none  [on_device(): lax.all_to_all(merged, 'fac', split_axis=0, concat_axis=0, tiled=True)]
    ppermute x4 -> x2, starting transfers between devices: 7.57 us -> 1.1 us  [border_shift(): return lax.ppermute(x, ('grp', 'fac'), pairs)]
    pallas_call x1, Pallas kernels: 25.5 us -> 19.5 us  [on_device(): pl.pallas_call(functools.partial(facet_kernel, group, ext), grid=(steps,)...]
    all_to_all x1 -> x0, starting transfers between devices: 4.06 us -> none  [on_device(): lax.all_to_all(merged, 'fac', split_axis=0, concat_axis=0, tiled=True)]
    pallas_call x1 -> x2, Pallas kernels: 2.82 us -> 5.51 us  [the longest x1 3.47 us: on_device(): pl.pallas_call(functools.partial(pack_kernel, per_step, ext), out_shape=p...]
    unnamed x10 -> x8, local copies, waits for them, and re-layouts: 2.9 us -> 0.7 us
    all_to_all x1, waiting for transfers between devices: 31.9 us -> 29.8 us  [on_device(): lax.all_to_all(packed, 'fac', split_axis=0, concat_axis=0, tiled=True)]
  transfers between devices with their start and end apart: 6 -> 3, of which waited for: 4 -> 3; matrix products, arithmetic and copies ran while one was open for 3% -> 4% of each run, Pallas kernels for 0% -> 0%
where the time goes in v2:
time: 120 us; the launch traced here: 118 us
  waiting for transfers between devices  37.5 us (31%)
  blocking collectives  36.8 us (31%)
  Pallas kernels  27.2 us (23%)
  starting transfers between devices  9.28 us (8%)
  local copies, waits for them, and re-layouts  3.5 us (3%)
  other arithmetic  2.29 us (2%)
  between operations  1.5 us (1%)
    all_to_all x1, blocking collectives, on_device(): lax.all_to_all(merged, 'fac', split_axis=0, concat_axis=0, tiled=True)  36.8 us
    all_to_all x1, waiting for transfers between devices, on_device(): lax.all_to_all(packed, 'fac', split_axis=0, concat_axis=0, tiled=True)  29.8 us
    pallas_call x1, Pallas kernels, on_device(): pl.pallas_call(functools.partial(facet_kernel, group, ext), grid=(steps,)...  19.5 us
    all_to_all x1, starting transfers between devices, on_device(): lax.all_to_all(packed, 'fac', split_axis=0, concat_axis=0, tiled=True)  8.17 us
    ppermute x2, waiting for transfers between devices, border_shift(): return lax.ppermute(x, ('grp', 'fac'), pairs)  7.71 us
    pallas_call x1, Pallas kernels, on_device(): pl.pallas_call(functools.partial(pack_kernel, per_step, ext), out_shape=p...  3.47 us
  transfers between devices with their start and end apart: 3, of which 3 were waited for; matrix products, arithmetic and copies ran while one was open for 4% of the time, Pallas kernels for 0%

profile of v2, /device:TPU:24, one launch (start us, length us, event | category | flops | bytes accessed | tf_op | source)
XLA Modules:
  0.0 118.1 jit_solution(2349518771098855391)
XLA Ops:
  0.6 0.7 copy-done
  1.3 3.5 %pack_facets.1 = f32[32,152,128]{2,1,0:T(8,128)} custom-call(s32[4,32]{1,0:T(4,128)S(1)} %copy-done, f32[1,1536,256]{2,1,0:T(8,128)} %image_ref.1), custom_call_target="tpu_custom_call" | custom-call | tf_op jit(solution)/shard_map/pack_facets/pallas_call | solution.py:272
  4.8 8.2 %all-to-all-start = ((f32[32,152,128]{2,1,0:T(8,128)}), f32[32,152,128]{2,1,0:T(8,128)S(1)}, u32[]{:S(2)}, u32[]{:S(2)}) async-start(f32[32,152,128]{2,1,0:T(8,128)} %pack_facets.1), calls=%async_computation | async-start | bytes 4980736 | tf_op jit(solution)/shard_map/all_to_all | solution.py:286
  13.0 0.6 dynamic_slice.13
  14.3 0.1 rev.3
  14.4 0.1 reshape.70.taps_ref
  14.5 0.1 fusion.8
  14.6 0.1 copy.16
  14.7 0.1 copy.17
  14.8 0.1 copy.18
  14.9 0.1 copy.19
  15.0 0.7 stack.47.info_ref
  16.1 0.7 add_convert_fusion
  16.8 0.9 slice_bitcast_fusion.1
  17.8 29.8 %all-to-all-done.x_hbm = f32[32,152,128]{2,1,0:T(8,128)S(1)} async-done(((f32[32,152,128]{2,1,0:T(8,128)}), f32[32,152,128]{2,1,0:T(8,128)S(1)}, u32[]{:S(2)}, u32[]{:S(2)}) %all-to-all-start) | async-done | bytes 2490400 | tf_op jit(solution)/shard_map/all_to_all | solution.py:286
  47.7 0.3 collective-permute-start
  48.0 1.1 pad_maximum_fusion.adj_ref
  49.0 3.0 %collective-permute-done.edge_ref = f32[32,4,128]{2,1,0:T(4,128)S(1)} collective-permute-done((f32[32,4,128]{2,1,0:T(4,128)S(1)}, f32[32,4,128]{2,1,0:T(4,128)S(1)}, u32[]{:S(2)}, u32[]{:S(2)}) %collective-permute-start) | collective-permute-done | bytes 65568 | tf_op jit(solution)/shard_map/ppermute | solution.py:22
  52.0 19.5 %facet_update.1 = (bf16[8,32,72,256]{3,2,1,0:T(8,128)(2,1)}, f32[32,152,128]{2,1,0:T(8,128)S(1)}, f32[32,4,128]{2,1,0:T(4,128)S(1)}) custom-call(f32[16]{0:T(128)S(1)} %reshape.70.taps_ref, f32[8]{0:T(128)S(1)} %copy-done.2, s32[5]{0:T(128)S(1)} %stack.47.info_ref, f32[32,4,128]{2,1,0:T(4,128)S(1)} %collective-permute-done.edge_ref, ...), custom_call_target="tpu_custom_call" | custom-call | tf_op jit(solution)/shard_map/facet_update/pallas_call | solution.py:306
  71.5 0.8 collective-permute-start.1
  72.3 4.7 %collective-permute-done.1.spill_ref = f32[32,4,128]{2,1,0:T(4,128)S(1)} collective-permute-done((f32[32,4,128]{2,1,0:T(4,128)S(1)}, f32[32,4,128]{2,1,0:T(4,128)S(1)}, u32[]{:S(2)}, u32[]{:S(2)}) %collective-permute-start.1) | collective-permute-done | bytes 65568 | tf_op jit(solution)/shard_map/ppermute | solution.py:22
  77.0 2.0 %add_border_rows.1 = f32[32,152,128]{2,1,0:T(8,128)} custom-call(s32[5]{0:T(128)S(1)} %stack.47.info_ref, f32[32,152,128]{2,1,0:T(8,128)S(1)} %get-tuple-element.6.merged_ref, f32[32,4,128]{2,1,0:T(4,128)S(1)} %collective-permute-done.1.spill_ref), custom_call_target="tpu_custom_call" | custom-call | tf_op jit(solution)/shard_map/add_border_rows/pallas_call | solution.py:332
  79.1 36.8 %all_to_all.10.block_ref = f32[32,152,128]{2,1,0:T(8,128)S(1)} all-to-all(f32[32,152,128]{2,1,0:T(8,128)} %add_border_rows.1), channel_id=1, replica_groups=mesh['grp'=4,'fac'=32] {'fac'}, dimensions={0} | all-to-all | bytes 4980736 | tf_op jit(solution)/shard_map/all_to_all | solution.py:341
  115.9 2.2 %unpack_facets.1 = f32[1,1536,256]{2,1,0:T(8,128)} custom-call(s32[4,32]{1,0:T(4,128)S(1)} %copy-done.1, f32[32,152,128]{2,1,0:T(8,128)S(1)} %all_to_all.10.block_ref), custom_call_target="tpu_custom_call" | custom-call | tf_op jit(solution)/shard_map/unpack_facets/pallas_call | solution.py:343
  (23 shorter events, 0.5 us)
Async XLA Ops:
  0.6 0.7 copy-start
  4.8 8.2 %copy-start.1 = (s32[4,32]{1,0:T(4,128)S(1)}, s32[4,32]{1,0:T(4,128)}, u32[]{:S(2)}) copy-start(s32[4,32]{1,0:T(4,128)} %rows_ref.3) | copy-start | bytes 1540
  4.8 9.5 %copy-start.3 = (bf16[2,4]{1,0:T(2,128)(2,1)S(1)}, bf16[2,4]{1,0:T(2,128)(2,1)}, u32[]{:S(2)}) copy-start(bf16[2,4]{1,0:T(2,128)(2,1)} %param.7) | copy-start | bytes 52
  4.8 42.8 %all-to-all-start = ((f32[32,152,128]{2,1,0:T(8,128)}), f32[32,152,128]{2,1,0:T(8,128)S(1)}, u32[]{:S(2)}, u32[]{:S(2)}) async-start(f32[32,152,128]{2,1,0:T(8,128)} %pack_facets.1), calls=%async_computation | async-start | bytes 4980736 | tf_op jit(solution)/shard_map/all_to_all | solution.py:286
  16.8 35.2 %copy-start.2 = (f32[8]{0:T(128)S(1)}, f32[8]{0:T(128)}, u32[]{:S(2)}) copy-start(f32[8]{0:T(128)} %thr_ref.1) | copy-start | bytes 100
  47.7 4.3 %collective-permute-start = (f32[32,4,128]{2,1,0:T(4,128)S(1)}, f32[32,4,128]{2,1,0:T(4,128)S(1)}, u32[]{:S(2)}, u32[]{:S(2)}) collective-permute-start(f32[32,4,128]{2,1,0:T(4,128)S(1)} %pad_maximum_fusion.1), channel_id=1, source_target_pairs={{0,32},{1,33},{2,34},{3,35},{4,36},{5,37},{6,38},{7,39},{8,40},{9,... | collective-permute-start | bytes 196616 | tf_op jit(solution)/shard_map/ppermute | solution.py:22
  71.5 5.5 %collective-permute-start.1 = (f32[32,4,128]{2,1,0:T(4,128)S(1)}, f32[32,4,128]{2,1,0:T(4,128)S(1)}, u32[]{:S(2)}, u32[]{:S(2)}) collective-permute-start(f32[32,4,128]{2,1,0:T(4,128)S(1)} %get-tuple-element.7), channel_id=1, source_target_pairs={{0,96},{1,97},{2,98},{3,99},{4,100},{5,101},{6,102},{7,103},{8,104... | collective-permute-start | bytes 196616 | tf_op jit(solution)/shard_map/ppermute | solution.py:22

commit v3 on v2

--- a/solution.py
+++ b/solution.py
@@ -17,7 +17,7 @@
     pairs = []
     for b in range(bands):
         for facet in range(facets):
-            to = b + by if facet < facets // 2 else b - by
+            to = b + by if facet % 2 == 0 else b - by
             pairs.append((b * facets + facet, (to % bands) * facets + facet))
     return lax.ppermute(x, ("grp", "fac"), pairs)
 
@@ -227,7 +227,7 @@
                 spill_ref[:, ABOVE * h : ABOVE * h + 1, :] = merged_ref[:, pl.ds(h * ext + ABOVE + length, 1), :]
 
 
-def border_kernel(ext, info_ref, merged_ref, spill_ref, out_ref, sem):
+def border_kernel(ext, info_ref, sent_ref, spill_ref, merged_ref):
     length, below, above = info_ref[0], info_ref[1], info_ref[2]
     inside = info_ref[4].astype(jnp.float32)
 
@@ -241,10 +241,6 @@
         for h in range(2):
             row = pl.ds(h * ext + ABOVE + length, 1)
             merged_ref[:, row, :] = inside * spill_ref[:, ABOVE * h : ABOVE * h + 1, :]
-
-    copy = pltpu.make_async_copy(merged_ref, out_ref, sem)
-    copy.start()
-    copy.wait()
 
 
 def on_device(image_cube, dual, lowpass, thresholds, facet_rows):
@@ -331,10 +327,10 @@
     spill = border_shift(spill, bands, facets, -1)
     merged = pl.pallas_call(
         functools.partial(border_kernel, ext),
-        out_shape=pltpu.HBM(received.shape, jnp.float32),
+        out_shape=jax.ShapeDtypeStruct(received.shape, jnp.float32),
         in_specs=[smem, vmem, vmem],
-        out_specs=hbm,
-        scratch_shapes=[pltpu.SemaphoreType.DMA],
+        out_specs=vmem,
+        input_output_aliases={1: 0},
         compiler_params=pltpu.CompilerParams(vmem_limit_bytes=16 << 20),
         name="add_border_rows",
     )(info, merged, spill)

time: 120 us -> 117 us (0.975)
  Pallas kernels: 27.2 us -> 25.7 us
    pallas_call x1, Pallas kernels: 2.04 us -> 0.57 us  [on_device(): pl.pallas_call(functools.partial(border_kernel, ext), out_shape=jax.Shape...]
where the time goes in v3:
time: 117 us; the launch traced here: 116 us
  waiting for transfers between devices  37.5 us (32%)
  blocking collectives  35.8 us (31%)
  Pallas kernels  25.7 us (22%)
  starting transfers between devices  9.28 us (8%)
  local copies, waits for them, and re-layouts  3.5 us (3%)
  other arithmetic  2.29 us (2%)
  between operations  1.5 us (1%)
    all_to_all x1, blocking collectives, on_device(): lax.all_to_all(merged, 'fac', split_axis=0, concat_axis=0, tiled=True)  35.8 us
    all_to_all x1, waiting for transfers between devices, on_device(): lax.all_to_all(packed, 'fac', split_axis=0, concat_axis=0, tiled=True)  29.8 us
    pallas_call x1, Pallas kernels, on_device(): pl.pallas_call(functools.partial(facet_kernel, group, ext), grid=(steps,)...  19.5 us
    all_to_all x1, starting transfers between devices, on_device(): lax.all_to_all(packed, 'fac', split_axis=0, concat_axis=0, tiled=True)  8.17 us
    ppermute x2, waiting for transfers between devices, border_shift(): return lax.ppermute(x, ('grp', 'fac'), pairs)  7.71 us
    pallas_call x1, Pallas kernels, on_device(): pl.pallas_call(functools.partial(pack_kernel, per_step, ext), out_shape=p...  3.47 us
  transfers between devices with their start and end apart: 3, of which 3 were waited for; matrix products, arithmetic and copies ran while one was open for 4% of the time, Pallas kernels for 0%

profile of v3, /device:TPU:24, one launch (start us, length us, event | category | flops | bytes accessed | tf_op | source)
XLA Modules:
  0.0 115.6 jit_solution(5883373636112003775)
XLA Ops:
  0.6 0.7 copy-done
  1.3 3.5 %pack_facets.1 = f32[32,152,128]{2,1,0:T(8,128)} custom-call(s32[4,32]{1,0:T(4,128)S(1)} %copy-done, f32[1,1536,256]{2,1,0:T(8,128)} %image_ref.1), custom_call_target="tpu_custom_call" | custom-call | tf_op jit(solution)/shard_map/pack_facets/pallas_call | solution.py:268
  4.8 8.2 %all-to-all-start = ((f32[32,152,128]{2,1,0:T(8,128)}), f32[32,152,128]{2,1,0:T(8,128)S(1)}, u32[]{:S(2)}, u32[]{:S(2)}) async-start(f32[32,152,128]{2,1,0:T(8,128)} %pack_facets.1), calls=%async_computation | async-start | bytes 4980736 | tf_op jit(solution)/shard_map/all_to_all | solution.py:282
  13.0 0.6 dynamic_slice.13
  14.3 0.1 rev.3
  14.4 0.1 reshape.70.taps_ref
  14.5 0.1 fusion.8
  14.6 0.1 copy.17
  14.7 0.1 copy.18
  14.8 0.1 copy.19
  14.9 0.1 copy.20
  15.0 0.7 stack.47.info_ref
  16.1 0.7 add_convert_fusion
  16.8 0.9 slice_bitcast_fusion.1
  17.8 29.8 %all-to-all-done.x_hbm = f32[32,152,128]{2,1,0:T(8,128)S(1)} async-done(((f32[32,152,128]{2,1,0:T(8,128)}), f32[32,152,128]{2,1,0:T(8,128)S(1)}, u32[]{:S(2)}, u32[]{:S(2)}) %all-to-all-start) | async-done | bytes 2490400 | tf_op jit(solution)/shard_map/all_to_all | solution.py:282
  47.7 0.3 collective-permute-start
  48.0 1.1 pad_maximum_fusion.adj_ref
  49.0 3.0 %collective-permute-done.edge_ref = f32[32,4,128]{2,1,0:T(4,128)S(1)} collective-permute-done((f32[32,4,128]{2,1,0:T(4,128)S(1)}, f32[32,4,128]{2,1,0:T(4,128)S(1)}, u32[]{:S(2)}, u32[]{:S(2)}) %collective-permute-start) | collective-permute-done | bytes 65568 | tf_op jit(solution)/shard_map/ppermute | solution.py:22
  52.0 19.5 %facet_update.1 = (bf16[8,32,72,256]{3,2,1,0:T(8,128)(2,1)}, f32[32,152,128]{2,1,0:T(8,128)S(1)}, f32[32,4,128]{2,1,0:T(4,128)S(1)}) custom-call(f32[16]{0:T(128)S(1)} %reshape.70.taps_ref, f32[8]{0:T(128)S(1)} %copy-done.2, s32[5]{0:T(128)S(1)} %stack.47.info_ref, f32[32,4,128]{2,1,0:T(4,128)S(1)} %collective-permute-done.edge_ref, ...), custom_call_target="tpu_custom_call" | custom-call | tf_op jit(solution)/shard_map/facet_update/pallas_call | solution.py:302
  71.5 0.8 collective-permute-start.1
  72.3 4.7 %collective-permute-done.1.spill_ref = f32[32,4,128]{2,1,0:T(4,128)S(1)} collective-permute-done((f32[32,4,128]{2,1,0:T(4,128)S(1)}, f32[32,4,128]{2,1,0:T(4,128)S(1)}, u32[]{:S(2)}, u32[]{:S(2)}) %collective-permute-start.1) | collective-permute-done | bytes 65568 | tf_op jit(solution)/shard_map/ppermute | solution.py:22
  77.0 0.6 add_border_rows.1
  77.6 35.8 %all_to_all.10.block_ref = f32[32,152,128]{2,1,0:T(8,128)S(1)} all-to-all(f32[32,152,128]{2,1,0:T(8,128)S(1)} %add_border_rows.1), channel_id=1, replica_groups=mesh['grp'=4,'fac'=32] {'fac'}, dimensions={0} | all-to-all | bytes 4980736 | tf_op jit(solution)/shard_map/all_to_all | solution.py:337
  113.4 2.2 %unpack_facets.1 = f32[1,1536,256]{2,1,0:T(8,128)} custom-call(s32[4,32]{1,0:T(4,128)S(1)} %copy-done.1, f32[32,152,128]{2,1,0:T(8,128)S(1)} %all_to_all.10.block_ref), custom_call_target="tpu_custom_call" | custom-call | tf_op jit(solution)/shard_map/unpack_facets/pallas_call | solution.py:339
  (23 shorter events, 0.5 us)
Async XLA Ops:
  0.6 0.7 copy-start
  4.8 8.2 %copy-start.1 = (s32[4,32]{1,0:T(4,128)S(1)}, s32[4,32]{1,0:T(4,128)}, u32[]{:S(2)}) copy-start(s32[4,32]{1,0:T(4,128)} %rows_ref.3) | copy-start | bytes 1540
  4.8 9.5 %copy-start.3 = (bf16[2,4]{1,0:T(2,128)(2,1)S(1)}, bf16[2,4]{1,0:T(2,128)(2,1)}, u32[]{:S(2)}) copy-start(bf16[2,4]{1,0:T(2,128)(2,1)} %param.7) | copy-start | bytes 52
  4.8 42.8 %all-to-all-start = ((f32[32,152,128]{2,1,0:T(8,128)}), f32[32,152,128]{2,1,0:T(8,128)S(1)}, u32[]{:S(2)}, u32[]{:S(2)}) async-start(f32[32,152,128]{2,1,0:T(8,128)} %pack_facets.1), calls=%async_computation | async-start | bytes 4980736 | tf_op jit(solution)/shard_map/all_to_all | solution.py:282
  16.8 35.2 %copy-start.2 = (f32[8]{0:T(128)S(1)}, f32[8]{0:T(128)}, u32[]{:S(2)}) copy-start(f32[8]{0:T(128)} %thr_ref.1) | copy-start | bytes 100
  47.7 4.3 %collective-permute-start = (f32[32,4,128]{2,1,0:T(4,128)S(1)}, f32[32,4,128]{2,1,0:T(4,128)S(1)}, u32[]{:S(2)}, u32[]{:S(2)}) collective-permute-start(f32[32,4,128]{2,1,0:T(4,128)S(1)} %pad_maximum_fusion.1), channel_id=1, source_target_pairs={{0,32},{1,97},{2,34},{3,99},{4,36},{5,101},{6,38},{7,103},{8,40},{... | collective-permute-start | bytes 196616 | tf_op jit(solution)/shard_map/ppermute | solution.py:22
  71.5 5.5 %collective-permute-start.1 = (f32[32,4,128]{2,1,0:T(4,128)S(1)}, f32[32,4,128]{2,1,0:T(4,128)S(1)}, u32[]{:S(2)}, u32[]{:S(2)}) collective-permute-start(f32[32,4,128]{2,1,0:T(4,128)S(1)} %get-tuple-element.7), channel_id=1, source_target_pairs={{0,96},{1,33},{2,98},{3,35},{4,100},{5,37},{6,102},{7,39},{8,104},... | collective-permute-start | bytes 196616 | tf_op jit(solution)/shard_map/ppermute | solution.py:22

commit v4 on v3

--- a/solution.py
+++ b/solution.py
@@ -49,30 +49,50 @@
     lax.fori_loop(0, facets, step, jnp.int32(0))
 
 
-def pack_kernel(per_copy, ext, rows_ref, image_ref, out_ref, strip, starts, blocks, in_sem, out_sem):
+def pack_kernel(per_copy, ext, rows_hbm, image_ref, out_ref, strip, starts, rows_ref, blocks, in_sem, out_sem):
     band_rows = image_ref.shape[1]
-    facets = rows_ref.shape[1]
+    facets = rows_hbm.shape[1]
+    steps = facets // per_copy
+    fetch_rows = pltpu.make_async_copy(rows_hbm, rows_ref, in_sem.at[2 * steps])
+    fetch_rows.start()
+    part = band_rows // steps
     copies = [
-        pltpu.make_async_copy(
-            image_ref.at[0, :, pl.ds(h * LANES, LANES)], strip.at[h, pl.ds(MARGIN, band_rows)], in_sem.at[h]
-        )
-        for h in range(2)
+        [
+            pltpu.make_async_copy(
+                image_ref.at[0, pl.ds(g * part, part), pl.ds(h * LANES, LANES)],
+                strip.at[h, pl.ds(MARGIN + g * part, part)],
+                in_sem.at[2 * g + h],
+            )
+            for h in range(2)
+        ]
+        for g in range(steps)
     ]
-    for copy in copies:
-        copy.start()
-    facet_starts(rows_ref, starts, facets)
+    for pair in copies[-1:] + copies[:-1]:
+        for copy in pair:
+            copy.start()
     end = MARGIN + band_rows
     for h in range(2):
         strip[h, 0:MARGIN] = jnp.zeros((MARGIN, LANES), jnp.float32)
         strip[h, end:] = jnp.zeros((strip.shape[1] - end, LANES), jnp.float32)
-    for copy in copies:
-        copy.wait()
+    fetch_rows.wait()
+    facet_starts(rows_ref, starts, facets)
+
+    def wait_for(g):
+        for copy in copies[g]:
+            copy.wait()
+
+    wait_for(steps - 1)
+    wait_for(0)
     for h in range(2):
         strip[h, MARGIN - ABOVE : MARGIN] = strip[h, end - ABOVE : end]
         strip[h, end : end + 1] = strip[h, MARGIN : MARGIN + 1]
 
+    arrived = 1
     outs = []
-    for g in range(facets // per_copy):
+    for g in range(steps):
+        while arrived < steps - 1 and arrived * part < (g + 1) * per_copy * (ext - TAPS) + TAPS:
+            wait_for(arrived)
+            arrived += 1
         for q in range(g * per_copy, (g + 1) * per_copy):
             begin = starts[q] + (MARGIN - ABOVE)
             for h in range(2):
@@ -123,8 +143,8 @@
             copy.wait()
 
 
-def facet_kernel(group, ext, taps_ref, thr_ref, info_ref, edge_ref, x_hbm, dual_ref, fwd_ref, adj_ref,
-                 next_ref, merged_ref, spill_ref, x_ref, u_ref, sq_ref, z_ref, in_sem):
+def facet_kernel(group, ext, taps_ref, thr_ref, info_ref, edge_ref, received_ref, dual_ref, fwd_ref, adj_ref,
+                 next_ref, merged_ref, spill_ref, x_ref, u_ref, sq_ref, z_ref):
     step = pl.program_id(0)
     channels, capacity, columns = dual_ref.shape[1:]
     dict_index = step // 2
@@ -133,57 +153,55 @@
     length, below, above = info_ref[0], info_ref[1], info_ref[2]
     inside = info_ref[3].astype(jnp.float32)
 
-    def incoming(i):
-        pick = pl.ds(i * group, group)
-        return pltpu.make_async_copy(x_hbm.at[pick], x_ref.at[pick], in_sem.at[i])
-
     @pl.when(step == 0)
     def _():
-        for i in range(channels // group):
-            incoming(i).start()
         merged_ref[...] = jnp.zeros_like(merged_ref)
         z_ref[...] = jnp.zeros_like(z_ref)
 
+        @pl.when(above == 1)
+        def _():
+            for h in range(2):
+                x_ref[:, h * ext : h * ext + ABOVE, :] = inside * edge_ref[:, ABOVE * h : ABOVE * (h + 1), :]
+
+        @pl.when(below == 1)
+        def _():
+            for h in range(2):
+                row = pl.ds(h * ext + ABOVE + length, 1)
+                x_ref[:, row, :] = inside * edge_ref[:, ABOVE * h : ABOVE * h + 1, :]
+
     sq_ref[...] = jnp.zeros_like(sq_ref)
 
-    def analyse(i, carry):
+    def analyse(i, begin, stop):
         pick = pl.ds(i * group, group)
 
-        @pl.when(step == 0)
-        def _():
-            incoming(i).wait()
-
-            @pl.when(above == 1)
-            def _():
-                for h in range(2):
-                    x_ref[pick, h * ext : h * ext + ABOVE, :] = inside * edge_ref[pick, ABOVE * h : ABOVE * (h + 1), :]
-
-            @pl.when(below == 1)
-            def _():
-                for h in range(2):
-                    row = pl.ds(h * ext + ABOVE + length, 1)
-                    x_ref[pick, row, :] = inside * edge_ref[pick, ABOVE * h : ABOVE * h + 1, :]
-
         halves = []
         for h in range(2):
-            total = taps[0] * x_ref[pick, h * ext : h * ext + capacity, :]
-            for k in range(1, TAPS):
+            total = taps[begin] * x_ref[pick, h * ext + begin : h * ext + begin + capacity, :]
+            for k in range(begin + 1, stop):
                 total = total + taps[k] * x_ref[pick, h * ext + k : h * ext + k + capacity, :]
             halves.append(total.reshape(rows, LANES))
         filtered = jnp.concatenate(halves, axis=1)
         high = filtered.astype(jnp.bfloat16)
         low = (filtered - high.astype(jnp.float32)).astype(jnp.bfloat16)
         coefficient = jnp.dot(
-            jnp.concatenate([high, low], axis=1), fwd_ref[dict_index], preferred_element_type=jnp.float32
+            jnp.concatenate([high, low], axis=1), fwd_ref[0], preferred_element_type=jnp.float32
         )
         for b in range(2):
             part = coefficient[:, b * columns : (b + 1) * columns].reshape(group, capacity, columns)
             combined = part + dual_ref[b, pick].astype(jnp.float32)
             u_ref[b, pick] = combined
             sq_ref[b] += jnp.sum(combined * combined, axis=0)
-        return carry
-
-    lax.fori_loop(0, channels // group, analyse, 0)
+
+    def over_groups(work):
+        @pl.when(dict_index == 0)
+        def _():
+            pl.loop(0, channels // group)(lambda i: work(i, 1, 3))
+
+        @pl.when(dict_index > 0)
+        def _():
+            pl.loop(0, channels // group)(lambda i: work(i, 0, TAPS))
+
+    over_groups(analyse)
 
     keep = lax.broadcasted_iota(jnp.int32, (capacity, columns), 0) < length
     for b in range(2):
@@ -191,26 +209,24 @@
         scale = radius / jnp.maximum(jnp.sqrt(sq_ref[b]), radius)
         sq_ref[b] = jnp.where(keep, scale, 0.0)
 
-    def synthesise(i, carry):
+    def synthesise(i, begin, stop):
         pick = pl.ds(i * group, group)
         parts = []
         for b in range(2):
             scaled = u_ref[b, pick] * sq_ref[b][None]
             next_ref[b, pick] = scaled.astype(jnp.bfloat16)
             parts.append(scaled.reshape(rows, columns).astype(jnp.bfloat16))
-        z = jnp.dot(jnp.concatenate(parts, axis=1), adj_ref[dict_index], preferred_element_type=jnp.float32)
+        z = jnp.dot(jnp.concatenate(parts, axis=1), adj_ref[0], preferred_element_type=jnp.float32)
         z = z.reshape(group, capacity, columns)
         for h in range(2):
             z_ref[h, :, 8 : 8 + capacity, :] = z[:, :, h * LANES : (h + 1) * LANES]
         for h in range(2):
-            total = taps[0] * z_ref[h, :, 8 : 8 + ext, :]
-            for k in range(1, TAPS):
+            total = taps[begin] * z_ref[h, :, 8 - begin : 8 - begin + ext, :]
+            for k in range(begin + 1, stop):
                 total = total + taps[k] * z_ref[h, :, 8 - k : 8 - k + ext, :]
             merged_ref[pick, h * ext : (h + 1) * ext, :] += total
 
-        return carry
-
-    lax.fori_loop(0, channels // group, synthesise, 0)
+    over_groups(synthesise)
 
     @pl.when(step == pl.num_programs(0) - 1)
     def _():
@@ -268,16 +284,17 @@
     packed = pl.pallas_call(
         functools.partial(pack_kernel, per_step, ext),
         out_shape=pltpu.HBM((facets, 2 * ext, LANES), jnp.float32),
-        in_specs=[smem, hbm],
+        in_specs=[hbm, hbm],
         out_specs=hbm,
         scratch_shapes=row_scratch[:2] + [
+            pltpu.SMEM(facet_rows.shape, jnp.int32),
             pltpu.VMEM((facets, 2 * ext, LANES), jnp.float32),
-            pltpu.SemaphoreType.DMA((2,)),
+            pltpu.SemaphoreType.DMA((2 * (facets // per_step) + 1,)),
             pltpu.SemaphoreType.DMA((facets // per_step,)),
         ],
         compiler_params=pltpu.CompilerParams(vmem_limit_bytes=16 << 20),
         name="pack_facets",
-    )(facet_rows, pltpu.with_memory_space_constraint(image_cube, pltpu.HBM))
+    )(*(pltpu.with_memory_space_constraint(a, pltpu.HBM) for a in (facet_rows, image_cube)))
 
     received = lax.all_to_all(packed, "fac", split_axis=0, concat_axis=0, tiled=True)
 
@@ -299,26 +316,26 @@
     edge_row = jnp.where(above, 0, own_length[0] + ABOVE)
     edges = [lax.dynamic_slice_in_dim(received, h * ext + edge_row, ABOVE, 1) for h in range(2)]
     edges = border_shift(jnp.concatenate(edges, axis=1), bands, facets, 1)
-    dual_next, merged, spill = pl.pallas_call(
+    dual_next, merged, spill, _ = pl.pallas_call(
         functools.partial(facet_kernel, group, ext),
         grid=(steps,),
         out_shape=(
             jax.ShapeDtypeStruct(dual.shape, jnp.bfloat16),
             jax.ShapeDtypeStruct(received.shape, jnp.float32),
             jax.ShapeDtypeStruct(edges.shape, jnp.float32),
+            jax.ShapeDtypeStruct(received.shape, jnp.float32),
         ),
         in_specs=[
-            smem, smem, smem, vmem, hbm, pair,
-            pl.BlockSpec(forward.shape, lambda i: (0, 0, 0)),
-            pl.BlockSpec(adjoint.shape, lambda i: (0, 0, 0)),
+            smem, smem, smem, vmem, vmem, pair,
+            pl.BlockSpec((1,) + forward.shape[1:], lambda i: (i // 2, 0, 0)),
+            pl.BlockSpec((1,) + adjoint.shape[1:], lambda i: (i // 2, 0, 0)),
         ],
-        out_specs=(pair, vmem, vmem),
+        out_specs=(pair, vmem, vmem, vmem),
+        input_output_aliases={4: 3},
         scratch_shapes=[
-            pltpu.VMEM((channels, 2 * ext, LANES), jnp.float32),
             pltpu.VMEM((2, channels, capacity, columns), jnp.float32),
             pltpu.VMEM((2, capacity, columns), jnp.float32),
             pltpu.VMEM((2, group, capacity + 16, LANES), jnp.float32),
-            pltpu.SemaphoreType.DMA((channels // group,)),
         ],
         compiler_params=pltpu.CompilerParams(vmem_limit_bytes=44 << 20),
         name="facet_update",

time: 117 us -> 114 us (0.974)
  Pallas kernels: 25.7 us -> 23.8 us
    pallas_call x1, Pallas kernels: 19.5 us -> 18.1 us  [on_device(): pl.pallas_call(functools.partial(facet_kernel, group, ext), grid=(steps,)...]
where the time goes in v4:
time: 114 us; the launch traced here: 113 us
  waiting for transfers between devices  37.5 us (33%)
  blocking collectives  35.8 us (31%)
  Pallas kernels  23.8 us (21%)
  starting transfers between devices  9.2 us (8%)
  local copies, waits for them, and re-layouts  2.82 us (2%)
  other arithmetic  2.29 us (2%)
  between operations  1.48 us (1%)
    all_to_all x1, blocking collectives, on_device(): lax.all_to_all(merged, 'fac', split_axis=0, concat_axis=0, tiled=True)  35.8 us
    all_to_all x1, waiting for transfers between devices, on_device(): lax.all_to_all(packed, 'fac', split_axis=0, concat_axis=0, tiled=True)  29.8 us
    pallas_call x1, Pallas kernels, on_device(): pl.pallas_call(functools.partial(facet_kernel, group, ext), grid=(steps,)...  18.1 us
    all_to_all x1, starting transfers between devices, on_device(): lax.all_to_all(packed, 'fac', split_axis=0, concat_axis=0, tiled=True)  8.18 us
    ppermute x2, waiting for transfers between devices, border_shift(): return lax.ppermute(x, ('grp', 'fac'), pairs)  7.72 us
    pallas_call x1, Pallas kernels, on_device(): pl.pallas_call(functools.partial(pack_kernel, per_step, ext), out_shape=p...  2.94 us
  transfers between devices with their start and end apart: 3, of which 3 were waited for; matrix products, arithmetic and copies ran while one was open for 4% of the time, Pallas kernels for 0%

profile of v4, /device:TPU:24, one launch (start us, length us, event | category | flops | bytes accessed | tf_op | source)
XLA Modules:
  0.0 112.9 jit_solution(8444859277581742008)
XLA Ops:
  0.6 2.9 %pack_facets.1 = f32[32,152,128]{2,1,0:T(8,128)} custom-call(s32[4,32]{1,0:T(4,128)} %rows_ref.1, f32[1,1536,256]{2,1,0:T(8,128)} %image_ref.1), custom_call_target="tpu_custom_call" | custom-call | tf_op jit(solution)/shard_map/pack_facets/pallas_call | solution.py:284
  3.6 8.2 %all-to-all-start = ((f32[32,152,128]{2,1,0:T(8,128)}), f32[32,152,128]{2,1,0:T(8,128)S(1)}, u32[]{:S(2)}, u32[]{:S(2)}) async-start(f32[32,152,128]{2,1,0:T(8,128)} %pack_facets.1), calls=%async_computation | async-start | bytes 4980736 | tf_op jit(solution)/shard_map/all_to_all | solution.py:299
  11.8 0.6 dynamic_slice.13
  13.1 0.1 rev.3
  13.2 0.1 reshape.70.taps_ref
  13.3 0.1 fusion.8
  13.4 0.1 copy.18
  13.5 0.1 copy.19
  13.6 0.1 copy.20
  13.7 0.1 copy.21
  13.8 0.7 stack.47.info_ref
  14.9 0.7 add_convert_fusion
  15.6 0.9 slice_bitcast_fusion.1
  16.5 0.1 maximum_maximum_fusion.fwd_ref
  16.5 29.8 %all-to-all-done.received_ref = f32[32,152,128]{2,1,0:T(8,128)S(1)} async-done(((f32[32,152,128]{2,1,0:T(8,128)}), f32[32,152,128]{2,1,0:T(8,128)S(1)}, u32[]{:S(2)}, u32[]{:S(2)}) %all-to-all-start) | async-done | bytes 2490400 | tf_op jit(solution)/shard_map/all_to_all | solution.py:299
  46.4 0.3 collective-permute-start
  46.7 1.1 pad_maximum_fusion.adj_ref
  47.8 3.0 %collective-permute-done.edge_ref = f32[32,4,128]{2,1,0:T(4,128)S(1)} collective-permute-done((f32[32,4,128]{2,1,0:T(4,128)S(1)}, f32[32,4,128]{2,1,0:T(4,128)S(1)}, u32[]{:S(2)}, u32[]{:S(2)}) %collective-permute-start) | collective-permute-done | bytes 65568 | tf_op jit(solution)/shard_map/ppermute | solution.py:22
  50.8 18.1 %facet_update.1 = (bf16[8,32,72,256]{3,2,1,0:T(8,128)(2,1)}, f32[32,152,128]{2,1,0:T(8,128)S(1)}, f32[32,4,128]{2,1,0:T(4,128)S(1)}, f32[32,152,128]{2,1,0:T(8,128)S(1)}) custom-call(f32[16]{0:T(128)S(1)} %reshape.70.taps_ref, f32[8]{0:T(128)S(1)} %copy-done.1, s32[5]{0:T(128)S(1)} %stack.47.info_ref, ...), custom_call_target="tpu_custom_call", output_to_operand_aliasing={{3}: (4, {})} | custom-call | tf_op jit(solution)/shard_map/facet_update/pallas_call | solution.py:319
  68.9 0.7 collective-permute-start.1
  69.6 4.7 %collective-permute-done.1.spill_ref = f32[32,4,128]{2,1,0:T(4,128)S(1)} collective-permute-done((f32[32,4,128]{2,1,0:T(4,128)S(1)}, f32[32,4,128]{2,1,0:T(4,128)S(1)}, u32[]{:S(2)}, u32[]{:S(2)}) %collective-permute-start.1) | collective-permute-done | bytes 65568 | tf_op jit(solution)/shard_map/ppermute | solution.py:22
  74.4 0.6 add_border_rows.1
  74.9 35.8 %all_to_all.10.block_ref = f32[32,152,128]{2,1,0:T(8,128)S(1)} all-to-all(f32[32,152,128]{2,1,0:T(8,128)S(1)} %add_border_rows.1), channel_id=1, replica_groups=mesh['grp'=4,'fac'=32] {'fac'}, dimensions={0} | all-to-all | bytes 4980736 | tf_op jit(solution)/shard_map/all_to_all | solution.py:354
  110.7 2.2 %unpack_facets.1 = f32[1,1536,256]{2,1,0:T(8,128)} custom-call(s32[4,32]{1,0:T(4,128)S(1)} %copy-done, f32[32,152,128]{2,1,0:T(8,128)S(1)} %all_to_all.10.block_ref), custom_call_target="tpu_custom_call" | custom-call | tf_op jit(solution)/shard_map/unpack_facets/pallas_call | solution.py:356
  (21 shorter events, 0.4 us)
Async XLA Ops:
  3.6 8.2 %copy-start = (s32[4,32]{1,0:T(4,128)S(1)}, s32[4,32]{1,0:T(4,128)}, u32[]{:S(2)}) copy-start(s32[4,32]{1,0:T(4,128)} %rows_ref.1) | copy-start | bytes 1540
  3.6 9.5 %copy-start.2 = (bf16[2,4]{1,0:T(2,128)(2,1)S(1)}, bf16[2,4]{1,0:T(2,128)(2,1)}, u32[]{:S(2)}) copy-start(bf16[2,4]{1,0:T(2,128)(2,1)} %param.7) | copy-start | bytes 52
  3.6 42.8 %all-to-all-start = ((f32[32,152,128]{2,1,0:T(8,128)}), f32[32,152,128]{2,1,0:T(8,128)S(1)}, u32[]{:S(2)}, u32[]{:S(2)}) async-start(f32[32,152,128]{2,1,0:T(8,128)} %pack_facets.1), calls=%async_computation | async-start | bytes 4980736 | tf_op jit(solution)/shard_map/all_to_all | solution.py:299
  15.6 35.2 %copy-start.1 = (f32[8]{0:T(128)S(1)}, f32[8]{0:T(128)}, u32[]{:S(2)}) copy-start(f32[8]{0:T(128)} %thr_ref.1) | copy-start | bytes 100
  46.4 4.3 %collective-permute-start = (f32[32,4,128]{2,1,0:T(4,128)S(1)}, f32[32,4,128]{2,1,0:T(4,128)S(1)}, u32[]{:S(2)}, u32[]{:S(2)}) collective-permute-start(f32[32,4,128]{2,1,0:T(4,128)S(1)} %pad_maximum_fusion.1), channel_id=1, source_target_pairs={{0,32},{1,97},{2,34},{3,99},{4,36},{5,101},{6,38},{7,103},{8,40},{... | collective-permute-start | bytes 196616 | tf_op jit(solution)/shard_map/ppermute | solution.py:22
  68.9 5.5 %collective-permute-start.1 = (f32[32,4,128]{2,1,0:T(4,128)S(1)}, f32[32,4,128]{2,1,0:T(4,128)S(1)}, u32[]{:S(2)}, u32[]{:S(2)}) collective-permute-start(f32[32,4,128]{2,1,0:T(4,128)S(1)} %get-tuple-element.7), channel_id=1, source_target_pairs={{0,96},{1,33},{2,98},{3,35},{4,100},{5,37},{6,102},{7,39},{8,104},... | collective-permute-start | bytes 196616 | tf_op jit(solution)/shard_map/ppermute | solution.py:22

commit v5 on v4

--- a/solution.py
+++ b/solution.py
@@ -104,49 +104,86 @@
         copy.wait()
 
 
-def unpack_kernel(per_step, ext, rows_ref, block_ref, out_ref, strip, starts, sem):
-    step = pl.program_id(0)
+def unpack_kernel(capacity, ext, rows_ref, block_ref, out_ref, strip, starts, sem):
     band_rows = out_ref.shape[1]
-    facets = rows_ref.shape[1]
-
-    @pl.when(step == 0)
-    def _():
-        facet_starts(rows_ref, starts, facets)
-        for h in range(2):
-            strip[h, 0 : 2 * MARGIN] = jnp.zeros((2 * MARGIN, LANES), jnp.float32)
+    facets = block_ref.shape[0]
+    end = MARGIN + band_rows
+    facet_starts(rows_ref, starts, facets)
+    for h in range(2):
+        strip[h, 0 : 2 * MARGIN] = jnp.zeros((2 * MARGIN, LANES), jnp.float32)
+
+    copies = []
+
+    def send(begin, stop):
+        for h in range(2):
+            copies.append(
+                pltpu.make_async_copy(
+                    strip.at[h, pl.ds(MARGIN + begin, stop - begin)],
+                    out_ref.at[0, pl.ds(begin, stop - begin), pl.ds(h * LANES, LANES)],
+                    sem.at[len(copies)],
+                )
+            )
+            copies[-1].start()
 
     shared = lax.broadcasted_iota(jnp.int32, (8, LANES), 0) < 3
-    for q in range(per_step):
-        begin = starts[step * per_step + q] + (MARGIN - ABOVE)
+    early = 3 * facets // 4
+    ready = (band_rows - (facets - early) * capacity) // 8 * 8 - 8
+    for q in range(facets):
+        if q == early:
+            send(8, ready)
+        begin = starts[q] + (MARGIN - ABOVE)
         for h in range(2):
             before = strip[h, pl.ds(begin, 8)]
             strip[h, pl.ds(begin, 8)] = block_ref[q, h * ext : h * ext + 8] + jnp.where(shared, before, 0.0)
             strip[h, pl.ds(begin + 8, ext - 8)] = block_ref[q, h * ext + 8 : (h + 1) * ext]
-
-    @pl.when(step == pl.num_programs(0) - 1)
-    def _():
-        copies = []
-        end = MARGIN + band_rows
-        for h in range(2):
-            strip[h, end - ABOVE : end] += strip[h, MARGIN - ABOVE : MARGIN]
-            strip[h, MARGIN : MARGIN + 1] += strip[h, end : end + 1]
-            copies.append(
-                pltpu.make_async_copy(
-                    strip.at[h, pl.ds(MARGIN, band_rows)],
-                    out_ref.at[0, :, pl.ds(h * LANES, LANES)],
-                    sem.at[h],
-                )
-            )
-        for copy in copies:
-            copy.start()
-        for copy in copies:
-            copy.wait()
-
-
-def facet_kernel(group, ext, taps_ref, thr_ref, info_ref, edge_ref, received_ref, dual_ref, fwd_ref, adj_ref,
-                 next_ref, merged_ref, spill_ref, x_ref, u_ref, sq_ref, z_ref):
+    for h in range(2):
+        strip[h, end - ABOVE : end] += strip[h, MARGIN - ABOVE : MARGIN]
+        strip[h, MARGIN : MARGIN + 1] += strip[h, end : end + 1]
+    send(0, 8)
+    send(ready, band_rows)
+    for copy in copies:
+        copy.wait()
+
+
+def stage_kernel(received_ref, dual_hbm, fwd_any, adj_any, first_ref, fwd_ref, adj_ref, sem):
+    pairs = ((dual_hbm.at[pl.ds(0, 2)], first_ref), (fwd_any, fwd_ref), (adj_any, adj_ref))
+    copies = [pltpu.make_async_copy(src, dst, sem.at[i]) for i, (src, dst) in enumerate(pairs)]
+    for copy in copies:
+        copy.start()
+    for copy in copies:
+        copy.wait()
+
+
+def tail_kernel(tail_ref, begun_hbm, next_hbm, done_ref, sem):
+    pair = tail_ref.shape[0]
+    copy = pltpu.make_async_copy(tail_ref, next_hbm.at[pl.ds(next_hbm.shape[0] - pair, pair)], sem)
+    copy.start()
+    done_ref[...] = jnp.zeros_like(done_ref)
+    copy.wait()
+
+
+def facet_kernel(group, ext, taps_ref, thr_ref, info_ref, edge_ref, received_ref, first_ref, dual_hbm, fwd_ref, adj_ref,
+                 next_hbm, tail_ref, merged_ref, spill_ref, x_ref,
+                 in_slots, out_slots, u_ref, sq_ref, z_ref, in_sem, out_sem):
     step = pl.program_id(0)
-    channels, capacity, columns = dual_ref.shape[1:]
+    steps = dual_hbm.shape[0] // 2
+    channels, capacity, columns = dual_hbm.shape[1:]
+    slot = lax.rem(step, 2)
+
+    def fetch(i, place):
+        return pltpu.make_async_copy(dual_hbm.at[pl.ds(2 * i, 2)], in_slots.at[place], in_sem.at[place])
+
+    def store(i, place):
+        return pltpu.make_async_copy(out_slots.at[place], next_hbm.at[pl.ds(2 * i, 2)], out_sem.at[place])
+
+    @pl.when(step > 0)
+    def _():
+        fetch(step, slot).wait()
+
+    @pl.when(step < steps - 1)
+    def _():
+        fetch(step + 1, 1 - slot).start()
+
     dict_index = step // 2
     taps = [taps_ref[step * TAPS + k] for k in range(TAPS)]
     rows = group * capacity
@@ -171,7 +208,7 @@
 
     sq_ref[...] = jnp.zeros_like(sq_ref)
 
-    def analyse(i, begin, stop):
+    def analyse(i, source, begin, stop):
         pick = pl.ds(i * group, group)
 
         halves = []
@@ -184,24 +221,22 @@
         high = filtered.astype(jnp.bfloat16)
         low = (filtered - high.astype(jnp.float32)).astype(jnp.bfloat16)
         coefficient = jnp.dot(
-            jnp.concatenate([high, low], axis=1), fwd_ref[0], preferred_element_type=jnp.float32
+            jnp.concatenate([high, low], axis=1), fwd_ref[dict_index], preferred_element_type=jnp.float32
         )
         for b in range(2):
             part = coefficient[:, b * columns : (b + 1) * columns].reshape(group, capacity, columns)
-            combined = part + dual_ref[b, pick].astype(jnp.float32)
+            combined = part + source[b, pick].astype(jnp.float32)
             u_ref[b, pick] = combined
             sq_ref[b] += jnp.sum(combined * combined, axis=0)
 
-    def over_groups(work):
-        @pl.when(dict_index == 0)
+    def over_groups(when, work, place, begin, stop):
+        @pl.when(when)
         def _():
-            pl.loop(0, channels // group)(lambda i: work(i, 1, 3))
-
-        @pl.when(dict_index > 0)
-        def _():
-            pl.loop(0, channels // group)(lambda i: work(i, 0, TAPS))
-
-    over_groups(analyse)
+            pl.loop(0, channels // group)(lambda i: work(i, place, begin, stop))
+
+    over_groups(step == 0, analyse, first_ref, 1, 3)
+    over_groups(step == 1, analyse, in_slots.at[1], 1, 3)
+    over_groups(step >= 2, analyse, in_slots.at[slot], 0, TAPS)
 
     keep = lax.broadcasted_iota(jnp.int32, (capacity, columns), 0) < length
     for b in range(2):
@@ -209,14 +244,14 @@
         scale = radius / jnp.maximum(jnp.sqrt(sq_ref[b]), radius)
         sq_ref[b] = jnp.where(keep, scale, 0.0)
 
-    def synthesise(i, begin, stop):
+    def synthesise(i, target, begin, stop):
         pick = pl.ds(i * group, group)
         parts = []
         for b in range(2):
             scaled = u_ref[b, pick] * sq_ref[b][None]
-            next_ref[b, pick] = scaled.astype(jnp.bfloat16)
+            target[b, pick] = scaled.astype(jnp.bfloat16)
             parts.append(scaled.reshape(rows, columns).astype(jnp.bfloat16))
-        z = jnp.dot(jnp.concatenate(parts, axis=1), adj_ref[0], preferred_element_type=jnp.float32)
+        z = jnp.dot(jnp.concatenate(parts, axis=1), adj_ref[dict_index], preferred_element_type=jnp.float32)
         z = z.reshape(group, capacity, columns)
         for h in range(2):
             z_ref[h, :, 8 : 8 + capacity, :] = z[:, :, h * LANES : (h + 1) * LANES]
@@ -226,7 +261,17 @@
                 total = total + taps[k] * z_ref[h, :, 8 - k : 8 - k + ext, :]
             merged_ref[pick, h * ext : (h + 1) * ext, :] += total
 
-    over_groups(synthesise)
+    @pl.when(step == 2)
+    def _():
+        store(0, 0).wait()
+
+    over_groups(step < 2, synthesise, out_slots.at[slot], 1, 3)
+    over_groups(jnp.logical_and(step >= 2, step < steps - 1), synthesise, out_slots.at[slot], 0, TAPS)
+    over_groups(step == steps - 1, synthesise, tail_ref, 0, TAPS)
+
+    @pl.when(step < steps - 1)
+    def _():
+        store(step, slot).start()
 
     @pl.when(step == pl.num_programs(0) - 1)
     def _():
@@ -242,8 +287,11 @@
             for h in range(2):
                 spill_ref[:, ABOVE * h : ABOVE * h + 1, :] = merged_ref[:, pl.ds(h * ext + ABOVE + length, 1), :]
 
-
-def border_kernel(ext, info_ref, sent_ref, spill_ref, merged_ref):
+        store(1, 1).wait()
+        store(2, 0).wait()
+
+
+def border_kernel(ext, info_ref, sent_ref, spill_ref, stored_ref, merged_ref):
     length, below, above = info_ref[0], info_ref[1], info_ref[2]
     inside = info_ref[4].astype(jnp.float32)
 
@@ -275,9 +323,7 @@
     row_scratch = [
         pltpu.VMEM((2, strip_rows, LANES), jnp.float32),
         pltpu.SMEM((facets,), jnp.int32),
-        pltpu.SemaphoreType.DMA((2,)),
     ]
-    blocks = pl.BlockSpec((per_step, 2 * ext, LANES), lambda i, *_: (i, 0, 0))
     smem = pl.BlockSpec(memory_space=pltpu.SMEM)
     vmem = pl.BlockSpec(memory_space=pltpu.VMEM)
     hbm = pl.BlockSpec(memory_space=pltpu.HBM)
@@ -305,8 +351,20 @@
     swapped = jnp.swapaxes(matrices, 2, 3)
     adjoint = jnp.concatenate([swapped[:, 0], swapped[:, 1]], axis=1)
     group = 16
-    steps = subbands // 2
-    pair = pl.BlockSpec((2, channels, capacity, columns), lambda i: (i, 0, 0, 0))
+    dual = pltpu.with_memory_space_constraint(dual, pltpu.HBM)
+    pair = (2,) + dual.shape[1:]
+    any_space = pl.BlockSpec(memory_space=pl.ANY)
+    first, forward, adjoint = pl.pallas_call(
+        stage_kernel,
+        out_shape=[
+            jax.ShapeDtypeStruct(shape, jnp.bfloat16) for shape in (pair, forward.shape, adjoint.shape)
+        ],
+        in_specs=[any_space, hbm, any_space, any_space],
+        out_specs=[vmem] * 3,
+        scratch_shapes=[pltpu.SemaphoreType.DMA((3,))],
+        compiler_params=pltpu.CompilerParams(vmem_limit_bytes=16 << 20),
+        name="stage_first_pair",
+    )(received, dual, forward, adjoint)
     below = facet == facets - 1
     above = facet == 0
     before = jnp.where(above, band > 0, band < bands - 1)
@@ -316,50 +374,60 @@
     edge_row = jnp.where(above, 0, own_length[0] + ABOVE)
     edges = [lax.dynamic_slice_in_dim(received, h * ext + edge_row, ABOVE, 1) for h in range(2)]
     edges = border_shift(jnp.concatenate(edges, axis=1), bands, facets, 1)
-    dual_next, merged, spill, _ = pl.pallas_call(
+    dual_next, tail, merged, spill, _ = pl.pallas_call(
         functools.partial(facet_kernel, group, ext),
-        grid=(steps,),
+        grid=(subbands // 2,),
         out_shape=(
-            jax.ShapeDtypeStruct(dual.shape, jnp.bfloat16),
+            pltpu.HBM(dual.shape, jnp.bfloat16),
+            jax.ShapeDtypeStruct(pair, jnp.bfloat16),
             jax.ShapeDtypeStruct(received.shape, jnp.float32),
             jax.ShapeDtypeStruct(edges.shape, jnp.float32),
             jax.ShapeDtypeStruct(received.shape, jnp.float32),
         ),
-        in_specs=[
-            smem, smem, smem, vmem, vmem, pair,
-            pl.BlockSpec((1,) + forward.shape[1:], lambda i: (i // 2, 0, 0)),
-            pl.BlockSpec((1,) + adjoint.shape[1:], lambda i: (i // 2, 0, 0)),
-        ],
-        out_specs=(pair, vmem, vmem, vmem),
-        input_output_aliases={4: 3},
+        in_specs=[smem, smem, smem, vmem, vmem, vmem, hbm, vmem, vmem],
+        out_specs=(hbm, vmem, vmem, vmem, vmem),
+        input_output_aliases={4: 4},
         scratch_shapes=[
+            pltpu.VMEM((2,) + pair, jnp.bfloat16),
+            pltpu.VMEM((2,) + pair, jnp.bfloat16),
             pltpu.VMEM((2, channels, capacity, columns), jnp.float32),
             pltpu.VMEM((2, capacity, columns), jnp.float32),
             pltpu.VMEM((2, group, capacity + 16, LANES), jnp.float32),
+            pltpu.SemaphoreType.DMA((2,)),
+            pltpu.SemaphoreType.DMA((2,)),
         ],
-        compiler_params=pltpu.CompilerParams(vmem_limit_bytes=44 << 20),
+        compiler_params=pltpu.CompilerParams(vmem_limit_bytes=36 << 20),
         name="facet_update",
-    )(taps.reshape(-1), thresholds, info, edges, received, dual, forward, adjoint)
+    )(taps.reshape(-1), thresholds, info, edges, received, first, dual, forward, adjoint)
 
     spill = border_shift(spill, bands, facets, -1)
+    dual_next, stored = pl.pallas_call(
+        tail_kernel,
+        out_shape=(pltpu.HBM(dual.shape, jnp.bfloat16), jax.ShapeDtypeStruct((8, LANES), jnp.float32)),
+        in_specs=[vmem, hbm],
+        out_specs=(hbm, vmem),
+        input_output_aliases={1: 0},
+        scratch_shapes=[pltpu.SemaphoreType.DMA],
+        compiler_params=pltpu.CompilerParams(vmem_limit_bytes=16 << 20),
+        name="store_last_pair",
+    )(tail, dual_next)
     merged = pl.pallas_call(
         functools.partial(border_kernel, ext),
         out_shape=jax.ShapeDtypeStruct(received.shape, jnp.float32),
-        in_specs=[smem, vmem, vmem],
+        in_specs=[smem, vmem, vmem, vmem],
         out_specs=vmem,
         input_output_aliases={1: 0},
         compiler_params=pltpu.CompilerParams(vmem_limit_bytes=16 << 20),
         name="add_border_rows",
-    )(info, merged, spill)
+    )(info, merged, spill, stored)
     returned = lax.all_to_all(merged, "fac", split_axis=0, concat_axis=0, tiled=True)
 
     prior_term = pl.pallas_call(
-        functools.partial(unpack_kernel, per_step, ext),
-        grid=(facets // per_step,),
+        functools.partial(unpack_kernel, capacity, ext),
         out_shape=jax.ShapeDtypeStruct(image_cube.shape, jnp.float32),
-        in_specs=[smem, blocks],
+        in_specs=[smem, vmem],
         out_specs=hbm,
-        scratch_shapes=row_scratch,
+        scratch_shapes=row_scratch[:2] + [pltpu.SemaphoreType.DMA((6,))],
         compiler_params=pltpu.CompilerParams(vmem_limit_bytes=16 << 20),
         name="unpack_facets",
     )(facet_rows, returned)

time: 114 us -> 112 us (0.982)
  waiting for transfers between devices: 37.5 us -> 34.4 us
    ppermute x2, waiting for transfers between devices: 7.72 us -> 4.56 us  [border_shift(): return lax.ppermute(x, ('grp', 'fac'), pairs)]
    pallas_call x2 -> x4, Pallas kernels: 20.3 us -> 20.7 us  [the longest x1 15.5 us: on_device(): pl.pallas_call(functools.partial(facet_kernel, group, ext), grid=(subband...]
  transfers between devices with their start and end apart: 3 -> 3, of which waited for: 3 -> 3; matrix products, arithmetic and copies ran while one was open for 4% -> 5% of each run, Pallas kernels for 0% -> 3%
where the time goes in v5:
time: 112 us; the launch traced here: 110 us
  blocking collectives  35.8 us (32%)
  waiting for transfers between devices  34.4 us (31%)
  Pallas kernels  24.3 us (22%)
  starting transfers between devices  9.29 us (8%)
  local copies, waits for them, and re-layouts  2.81 us (3%)
  other arithmetic  2.3 us (2%)
  between operations  1.5 us (1%)
    all_to_all x1, blocking collectives, on_device(): lax.all_to_all(merged, 'fac', split_axis=0, concat_axis=0, tiled=True)  35.8 us
    all_to_all x1, waiting for transfers between devices, on_device(): lax.all_to_all(packed, 'fac', split_axis=0, concat_axis=0, tiled=True)  29.8 us
    pallas_call x1, Pallas kernels, on_device(): pl.pallas_call(functools.partial(facet_kernel, group, ext), grid=(subband...  15.5 us
    all_to_all x1, starting transfers between devices, on_device(): lax.all_to_all(packed, 'fac', split_axis=0, concat_axis=0, tiled=True)  8.18 us
    ppermute x2, waiting for transfers between devices, border_shift(): return lax.ppermute(x, ('grp', 'fac'), pairs)  4.56 us
    pallas_call x1, Pallas kernels, on_device(): pl.pallas_call(functools.partial(pack_kernel, per_step, ext), out_shape=p...  2.94 us
  transfers between devices with their start and end apart: 3, of which 3 were waited for; matrix products, arithmetic and copies ran while one was open for 5% of the time, Pallas kernels for 3%

profile of v5, /device:TPU:24, one launch (start us, length us, event | category | flops | bytes accessed | tf_op | source)
XLA Modules:
  0.0 110.3 jit_solution(15215396058905085768)
XLA Ops:
  0.6 2.9 %pack_facets.1 = f32[32,152,128]{2,1,0:T(8,128)} custom-call(s32[4,32]{1,0:T(4,128)} %rows_ref.1, f32[1,1536,256]{2,1,0:T(8,128)} %image_ref.1), custom_call_target="tpu_custom_call" | custom-call | tf_op jit(solution)/shard_map/pack_facets/pallas_call | solution.py:330
  3.6 8.2 %all-to-all-start = ((f32[32,152,128]{2,1,0:T(8,128)}), f32[32,152,128]{2,1,0:T(8,128)S(1)}, u32[]{:S(2)}, u32[]{:S(2)}) async-start(f32[32,152,128]{2,1,0:T(8,128)} %pack_facets.1), calls=%async_computation | async-start | bytes 4980736 | tf_op jit(solution)/shard_map/all_to_all | solution.py:345
  11.8 0.6 dynamic_slice.13
  13.1 0.1 rev.3
  13.2 0.1 reshape.70.taps_ref
  13.4 0.1 copy.19
  13.5 0.1 copy.20
  13.6 0.1 copy.21
  13.7 0.1 copy.22
  13.8 0.7 stack.47.info_ref
  14.9 0.7 add_convert_fusion
  15.6 0.9 slice_bitcast_fusion.1
  16.5 29.8 %all-to-all-done.received_ref = f32[32,152,128]{2,1,0:T(8,128)S(1)} async-done(((f32[32,152,128]{2,1,0:T(8,128)}), f32[32,152,128]{2,1,0:T(8,128)S(1)}, u32[]{:S(2)}, u32[]{:S(2)}) %all-to-all-start) | async-done | bytes 2490400 | tf_op jit(solution)/shard_map/all_to_all | solution.py:345
  46.5 0.3 collective-permute-start
  46.7 1.1 pad_maximum_fusion.adj_any
  47.8 1.7 %stage_first_pair.1 = (bf16[2,32,72,256]{3,2,1,0:T(8,128)(2,1)S(1)}, bf16[2,512,512]{2,1,0:T(8,128)(2,1)S(1)}, bf16[2,512,256]{2,1,0:T(8,128)(2,1)S(1)}) custom-call(f32[32,152,128]{2,1,0:T(8,128)S(1)} %all-to-all-done.received_ref, bf16[8,32,72,256]{3,2,1,0:T(8,128)(2,1)} %dual_hbm.3, bf16[2,512,512]{2,1,0:T(8,128)(2,1)S(1)} %maximum_maximum_fusion.fwd_any, ...), custom_call_target="tpu_custom_call" | custom-call | tf_op jit(solution)/shard_map/stage_first_pair/pallas_call | solution.py:357
  49.5 1.3 %collective-permute-done.edge_ref = f32[32,4,128]{2,1,0:T(4,128)S(1)} collective-permute-done((f32[32,4,128]{2,1,0:T(4,128)S(1)}, f32[32,4,128]{2,1,0:T(4,128)S(1)}, u32[]{:S(2)}, u32[]{:S(2)}) %collective-permute-start) | collective-permute-done | bytes 65568 | tf_op jit(solution)/shard_map/ppermute | solution.py:22
  50.8 15.5 %facet_update.1 = (bf16[8,32,72,256]{3,2,1,0:T(8,128)(2,1)}, bf16[2,32,72,256]{3,2,1,0:T(8,128)(2,1)S(1)}, f32[32,152,128]{2,1,0:T(8,128)S(1)}, f32[32,4,128]{2,1,0:T(4,128)S(1)}, f32[32,152,128]{2,1,0:T(8,128)S(1)}) custom-call(f32[16]{0:T(128)S(1)} %reshape.70.taps_ref, f32[8]{0:T(128)S(1)} %copy-done.1, ...), custom_call_target="tpu_custom_call", output_to_operand_aliasing={{4}: (4, {})} | custom-call | tf_op jit(solution)/shard_map/facet_update/pallas_call | solution.py:377
  66.3 0.8 collective-permute-start.1
  67.1 1.4 %store_last_pair.1 = (bf16[8,32,72,256]{3,2,1,0:T(8,128)(2,1)}, f32[8,128]{1,0:T(8,128)S(1)}) custom-call(bf16[2,32,72,256]{3,2,1,0:T(8,128)(2,1)S(1)} %get-tuple-element.14.tail_ref, bf16[8,32,72,256]{3,2,1,0:T(8,128)(2,1)} %get-tuple-element.15.begun_hbm), custom_call_target="tpu_custom_call", output_to_operand_aliasing={{0}: (1, {})} | custom-call | tf_op jit(solution)/shard_map/store_last_pair/pallas_call | solution.py:404
  68.5 3.3 %collective-permute-done.1.spill_ref = f32[32,4,128]{2,1,0:T(4,128)S(1)} collective-permute-done((f32[32,4,128]{2,1,0:T(4,128)S(1)}, f32[32,4,128]{2,1,0:T(4,128)S(1)}, u32[]{:S(2)}, u32[]{:S(2)}) %collective-permute-start.1) | collective-permute-done | bytes 65568 | tf_op jit(solution)/shard_map/ppermute | solution.py:22
  71.8 0.6 add_border_rows.1
  72.4 35.8 %all_to_all.10.block_ref = f32[32,152,128]{2,1,0:T(8,128)S(1)} all-to-all(f32[32,152,128]{2,1,0:T(8,128)S(1)} %add_border_rows.1), channel_id=1, replica_groups=mesh['grp'=4,'fac'=32] {'fac'}, dimensions={0} | all-to-all | bytes 4980736 | tf_op jit(solution)/shard_map/all_to_all | solution.py:423
  108.2 2.1 %unpack_facets.1 = f32[1,1536,256]{2,1,0:T(8,128)} custom-call(s32[4,32]{1,0:T(4,128)S(1)} %copy-done, f32[32,152,128]{2,1,0:T(8,128)S(1)} %all_to_all.10.block_ref), custom_call_target="tpu_custom_call" | custom-call | tf_op jit(solution)/shard_map/unpack_facets/pallas_call | solution.py:425
  (23 shorter events, 0.6 us)
Async XLA Ops:
  3.6 8.2 %copy-start = (s32[4,32]{1,0:T(4,128)S(1)}, s32[4,32]{1,0:T(4,128)}, u32[]{:S(2)}) copy-start(s32[4,32]{1,0:T(4,128)} %rows_ref.1) | copy-start | bytes 1540
  3.6 9.5 %copy-start.2 = (bf16[2,4]{1,0:T(2,128)(2,1)S(1)}, bf16[2,4]{1,0:T(2,128)(2,1)}, u32[]{:S(2)}) copy-start(bf16[2,4]{1,0:T(2,128)(2,1)} %param.7) | copy-start | bytes 52
  3.6 42.8 %all-to-all-start = ((f32[32,152,128]{2,1,0:T(8,128)}), f32[32,152,128]{2,1,0:T(8,128)S(1)}, u32[]{:S(2)}, u32[]{:S(2)}) async-start(f32[32,152,128]{2,1,0:T(8,128)} %pack_facets.1), calls=%async_computation | async-start | bytes 4980736 | tf_op jit(solution)/shard_map/all_to_all | solution.py:345
  46.5 4.3 %collective-permute-start = (f32[32,4,128]{2,1,0:T(4,128)S(1)}, f32[32,4,128]{2,1,0:T(4,128)S(1)}, u32[]{:S(2)}, u32[]{:S(2)}) collective-permute-start(f32[32,4,128]{2,1,0:T(4,128)S(1)} %pad_maximum_fusion.1), channel_id=1, source_target_pairs={{0,32},{1,97},{2,34},{3,99},{4,36},{5,101},{6,38},{7,103},{8,40},{... | collective-permute-start | bytes 196616 | tf_op jit(solution)/shard_map/ppermute | solution.py:22
  47.8 3.0 %copy-start.1 = (f32[8]{0:T(128)S(1)}, f32[8]{0:T(128)}, u32[]{:S(2)}) copy-start(f32[8]{0:T(128)} %thr_ref.1) | copy-start | bytes 100
  66.3 5.5 %collective-permute-start.1 = (f32[32,4,128]{2,1,0:T(4,128)S(1)}, f32[32,4,128]{2,1,0:T(4,128)S(1)}, u32[]{:S(2)}, u32[]{:S(2)}) collective-permute-start(f32[32,4,128]{2,1,0:T(4,128)S(1)} %get-tuple-element.18), channel_id=1, source_target_pairs={{0,96},{1,33},{2,98},{3,35},{4,100},{5,37},{6,102},{7,39},{8,104},... | collective-permute-start | bytes 196616 | tf_op jit(solution)/shard_map/ppermute | solution.py:22

commit v6 on v5

--- a/solution.py
+++ b/solution.py
@@ -165,52 +165,41 @@
 def facet_kernel(group, ext, taps_ref, thr_ref, info_ref, edge_ref, received_ref, first_ref, dual_hbm, fwd_ref, adj_ref,
                  next_hbm, tail_ref, merged_ref, spill_ref, x_ref,
                  in_slots, out_slots, u_ref, sq_ref, z_ref, in_sem, out_sem):
-    step = pl.program_id(0)
     steps = dual_hbm.shape[0] // 2
     channels, capacity, columns = dual_hbm.shape[1:]
-    slot = lax.rem(step, 2)
-
-    def fetch(i, place):
-        return pltpu.make_async_copy(dual_hbm.at[pl.ds(2 * i, 2)], in_slots.at[place], in_sem.at[place])
-
-    def store(i, place):
-        return pltpu.make_async_copy(out_slots.at[place], next_hbm.at[pl.ds(2 * i, 2)], out_sem.at[place])
-
-    @pl.when(step > 0)
-    def _():
-        fetch(step, slot).wait()
-
-    @pl.when(step < steps - 1)
-    def _():
-        fetch(step + 1, 1 - slot).start()
-
-    dict_index = step // 2
-    taps = [taps_ref[step * TAPS + k] for k in range(TAPS)]
     rows = group * capacity
     length, below, above = info_ref[0], info_ref[1], info_ref[2]
     inside = info_ref[3].astype(jnp.float32)
-
-    @pl.when(step == 0)
-    def _():
-        merged_ref[...] = jnp.zeros_like(merged_ref)
-        z_ref[...] = jnp.zeros_like(z_ref)
-
-        @pl.when(above == 1)
-        def _():
-            for h in range(2):
-                x_ref[:, h * ext : h * ext + ABOVE, :] = inside * edge_ref[:, ABOVE * h : ABOVE * (h + 1), :]
-
-        @pl.when(below == 1)
-        def _():
-            for h in range(2):
-                row = pl.ds(h * ext + ABOVE + length, 1)
-                x_ref[:, row, :] = inside * edge_ref[:, ABOVE * h : ABOVE * h + 1, :]
-
-    sq_ref[...] = jnp.zeros_like(sq_ref)
-
-    def analyse(i, source, begin, stop):
+    spans = [(1, 3) if step < steps // 2 else (0, TAPS) for step in range(steps)]
+    sources = [first_ref] + [in_slots.at[step % 2] for step in range(1, steps)]
+    targets = [out_slots.at[step % 2] for step in range(steps - 1)] + [tail_ref]
+    fetches = [
+        pltpu.make_async_copy(dual_hbm.at[pl.ds(2 * step, 2)], in_slots.at[step % 2], in_sem.at[step % 2])
+        for step in range(steps)
+    ]
+    stores = [
+        pltpu.make_async_copy(out_slots.at[step % 2], next_hbm.at[pl.ds(2 * step, 2)], out_sem.at[step % 2])
+        for step in range(steps)
+    ]
+    for step in range(1, 3):
+        fetches[step].start()
+    z_ref[...] = jnp.zeros_like(z_ref)
+
+    @pl.when(above == 1)
+    def _():
+        for h in range(2):
+            x_ref[:, h * ext : h * ext + ABOVE, :] = inside * edge_ref[:, ABOVE * h : ABOVE * (h + 1), :]
+
+    @pl.when(below == 1)
+    def _():
+        for h in range(2):
+            row = pl.ds(h * ext + ABOVE + length, 1)
+            x_ref[:, row, :] = inside * edge_ref[:, ABOVE * h : ABOVE * h + 1, :]
+
+    def analyse(step, i):
         pick = pl.ds(i * group, group)
-
+        begin, stop = spans[step]
+        taps = [taps_ref[step * TAPS + k] for k in range(TAPS)]
         halves = []
         for h in range(2):
             total = taps[begin] * x_ref[pick, h * ext + begin : h * ext + begin + capacity, :]
@@ -221,37 +210,24 @@
         high = filtered.astype(jnp.bfloat16)
         low = (filtered - high.astype(jnp.float32)).astype(jnp.bfloat16)
         coefficient = jnp.dot(
-            jnp.concatenate([high, low], axis=1), fwd_ref[dict_index], preferred_element_type=jnp.float32
+            jnp.concatenate([high, low], axis=1), fwd_ref[step // 2], preferred_element_type=jnp.float32
         )
         for b in range(2):
             part = coefficient[:, b * columns : (b + 1) * columns].reshape(group, capacity, columns)
-            combined = part + source[b, pick].astype(jnp.float32)
-            u_ref[b, pick] = combined
-            sq_ref[b] += jnp.sum(combined * combined, axis=0)
-
-    def over_groups(when, work, place, begin, stop):
-        @pl.when(when)
-        def _():
-            pl.loop(0, channels // group)(lambda i: work(i, place, begin, stop))
-
-    over_groups(step == 0, analyse, first_ref, 1, 3)
-    over_groups(step == 1, analyse, in_slots.at[1], 1, 3)
-    over_groups(step >= 2, analyse, in_slots.at[slot], 0, TAPS)
-
-    keep = lax.broadcasted_iota(jnp.int32, (capacity, columns), 0) < length
-    for b in range(2):
-        radius = thr_ref[step * 2 + b]
-        scale = radius / jnp.maximum(jnp.sqrt(sq_ref[b]), radius)
-        sq_ref[b] = jnp.where(keep, scale, 0.0)
-
-    def synthesise(i, target, begin, stop):
+            combined = part + sources[step][b, pick].astype(jnp.float32)
+            u_ref[step % 2, b, pick] = combined
+            sq_ref[step % 2, b] += jnp.sum(combined * combined, axis=0)
+
+    def synthesise(step, i):
         pick = pl.ds(i * group, group)
+        begin, stop = spans[step]
+        taps = [taps_ref[step * TAPS + k] for k in range(TAPS)]
         parts = []
         for b in range(2):
-            scaled = u_ref[b, pick] * sq_ref[b][None]
-            target[b, pick] = scaled.astype(jnp.bfloat16)
+            scaled = u_ref[step % 2, b, pick] * sq_ref[step % 2, b][None]
+            targets[step][b, pick] = scaled.astype(jnp.bfloat16)
             parts.append(scaled.reshape(rows, columns).astype(jnp.bfloat16))
-        z = jnp.dot(jnp.concatenate(parts, axis=1), adj_ref[dict_index], preferred_element_type=jnp.float32)
+        z = jnp.dot(jnp.concatenate(parts, axis=1), adj_ref[step // 2], preferred_element_type=jnp.float32)
         z = z.reshape(group, capacity, columns)
         for h in range(2):
             z_ref[h, :, 8 : 8 + capacity, :] = z[:, :, h * LANES : (h + 1) * LANES]
@@ -259,36 +235,55 @@
             total = taps[begin] * z_ref[h, :, 8 - begin : 8 - begin + ext, :]
             for k in range(begin + 1, stop):
                 total = total + taps[k] * z_ref[h, :, 8 - k : 8 - k + ext, :]
-            merged_ref[pick, h * ext : (h + 1) * ext, :] += total
-
-    @pl.when(step == 2)
-    def _():
-        store(0, 0).wait()
-
-    over_groups(step < 2, synthesise, out_slots.at[slot], 1, 3)
-    over_groups(jnp.logical_and(step >= 2, step < steps - 1), synthesise, out_slots.at[slot], 0, TAPS)
-    over_groups(step == steps - 1, synthesise, tail_ref, 0, TAPS)
-
-    @pl.when(step < steps - 1)
-    def _():
-        store(step, slot).start()
-
-    @pl.when(step == pl.num_programs(0) - 1)
-    def _():
-        spill_ref[...] = jnp.zeros_like(spill_ref)
-
-        @pl.when(above == 1)
-        def _():
-            for h in range(2):
-                spill_ref[:, ABOVE * h : ABOVE * (h + 1), :] = merged_ref[:, h * ext : h * ext + ABOVE, :]
-
-        @pl.when(below == 1)
-        def _():
-            for h in range(2):
-                spill_ref[:, ABOVE * h : ABOVE * h + 1, :] = merged_ref[:, pl.ds(h * ext + ABOVE + length, 1), :]
-
-        store(1, 1).wait()
-        store(2, 0).wait()
+            if step == 0:
+                merged_ref[pick, h * ext : (h + 1) * ext, :] = total
+            else:
+                merged_ref[pick, h * ext : (h + 1) * ext, :] += total
+
+    keep = lax.broadcasted_iota(jnp.int32, (capacity, columns), 0) < length
+    for stage in range(steps + 1):
+        if 0 < stage < steps:
+            fetches[stage].wait()
+        if stage == 3:
+            stores[0].wait()
+        if stage < steps:
+            sq_ref[stage % 2] = jnp.zeros_like(sq_ref[stage % 2])
+
+        def work(i):
+            if stage > 0:
+                synthesise(stage - 1, i)
+            if stage < steps:
+                analyse(stage, i)
+
+        if stage > 0:
+            pl.loop(0, channels // group)(lambda i: synthesise(stage - 1, i))
+        if stage < steps:
+            pl.loop(0, channels // group)(lambda i: analyse(stage, i))
+        if stage == 1:
+            fetches[3].start()
+        if 0 < stage < steps:
+            stores[stage - 1].start()
+        if stage < steps:
+            for b in range(2):
+                radius = thr_ref[stage * 2 + b]
+                scale = radius / jnp.maximum(jnp.sqrt(sq_ref[stage % 2, b]), radius)
+                sq_ref[stage % 2, b] = jnp.where(keep, scale, 0.0)
+
+    spill_ref[...] = jnp.zeros_like(spill_ref)
+
+    @pl.when(above == 1)
+    def _():
+        for h in range(2):
+            spill_ref[:, ABOVE * h : ABOVE * (h + 1), :] = merged_ref[:, h * ext : h * ext + ABOVE, :]
+
+    @pl.when(below == 1)
+    def _():
+        for h in range(2):
+            row = pl.ds(h * ext + ABOVE + length, 1)
+            spill_ref[:, ABOVE * h : ABOVE * h + 1, :] = merged_ref[:, row, :]
+
+    stores[1].wait()
+    stores[2].wait()
 
 
 def border_kernel(ext, info_ref, sent_ref, spill_ref, stored_ref, merged_ref):
@@ -315,7 +310,7 @@
     _, band_rows, columns = image_cube.shape
     subbands, channels, capacity, _ = dual.shape
     ext = capacity + TAPS
-    per_step = 8
+    per_step = 4
     strip_rows = MARGIN + band_rows + capacity
     lengths = lax.dynamic_index_in_dim(facet_rows, band, 0, keepdims=False)
     own_length = lax.dynamic_slice_in_dim(lengths, facet, 1)
@@ -376,7 +371,6 @@
     edges = border_shift(jnp.concatenate(edges, axis=1), bands, facets, 1)
     dual_next, tail, merged, spill, _ = pl.pallas_call(
         functools.partial(facet_kernel, group, ext),
-        grid=(subbands // 2,),
         out_shape=(
             pltpu.HBM(dual.shape, jnp.bfloat16),
             jax.ShapeDtypeStruct(pair, jnp.bfloat16),
@@ -390,8 +384,8 @@
         scratch_shapes=[
             pltpu.VMEM((2,) + pair, jnp.bfloat16),
             pltpu.VMEM((2,) + pair, jnp.bfloat16),
-            pltpu.VMEM((2, channels, capacity, columns), jnp.float32),
-            pltpu.VMEM((2, capacity, columns), jnp.float32),
+            pltpu.VMEM((2, 2, channels, capacity, columns), jnp.float32),
+            pltpu.VMEM((2, 2, capacity, columns), jnp.float32),
             pltpu.VMEM((2, group, capacity + 16, LANES), jnp.float32),
             pltpu.SemaphoreType.DMA((2,)),
             pltpu.SemaphoreType.DMA((2,)),

time: 112 us -> 111 us (level)
  no operation moved by 1% of the time
where the time goes in v6:
time: 111 us; the launch traced here: 110 us
  blocking collectives  35.8 us (32%)
  waiting for transfers between devices  34.4 us (31%)
  Pallas kernels  23.8 us (21%)
  starting transfers between devices  9.28 us (8%)
  local copies, waits for them, and re-layouts  2.81 us (3%)
  other arithmetic  2.3 us (2%)
  between operations  1.5 us (1%)
    all_to_all x1, blocking collectives, on_device(): lax.all_to_all(merged, 'fac', split_axis=0, concat_axis=0, tiled=True)  35.8 us
    all_to_all x1, waiting for transfers between devices, on_device(): lax.all_to_all(packed, 'fac', split_axis=0, concat_axis=0, tiled=True)  29.8 us
    pallas_call x1, Pallas kernels, on_device(): pl.pallas_call(functools.partial(facet_kernel, group, ext), out_shape=(pl...  15.1 us
    all_to_all x1, starting transfers between devices, on_device(): lax.all_to_all(packed, 'fac', split_axis=0, concat_axis=0, tiled=True)  8.18 us
    ppermute x2, waiting for transfers between devices, border_shift(): return lax.ppermute(x, ('grp', 'fac'), pairs)  4.57 us
    pallas_call x1, Pallas kernels, on_device(): pl.pallas_call(functools.partial(pack_kernel, per_step, ext), out_shape=p...  2.85 us
  transfers between devices with their start and end apart: 3, of which 3 were waited for; matrix products, arithmetic and copies ran while one was open for 5% of the time, Pallas kernels for 3%

profile of v6, /device:TPU:24, one launch (start us, length us, event | category | flops | bytes accessed | tf_op | source)
XLA Modules:
  0.0 109.8 jit_solution(13187390117934693851)
XLA Ops:
  0.6 2.8 %pack_facets.1 = f32[32,152,128]{2,1,0:T(8,128)} custom-call(s32[4,32]{1,0:T(4,128)} %rows_ref.1, f32[1,1536,256]{2,1,0:T(8,128)} %image_ref.1), custom_call_target="tpu_custom_call" | custom-call | tf_op jit(solution)/shard_map/pack_facets/pallas_call | solution.py:325
  3.5 8.2 %all-to-all-start = ((f32[32,152,128]{2,1,0:T(8,128)}), f32[32,152,128]{2,1,0:T(8,128)S(1)}, u32[]{:S(2)}, u32[]{:S(2)}) async-start(f32[32,152,128]{2,1,0:T(8,128)} %pack_facets.1), calls=%async_computation | async-start | bytes 4980736 | tf_op jit(solution)/shard_map/all_to_all | solution.py:340
  11.7 0.6 dynamic_slice.13
  13.0 0.1 rev.3
  13.1 0.1 reshape.70.taps_ref
  13.3 0.1 copy.19
  13.4 0.1 copy.20
  13.5 0.1 copy.21
  13.6 0.1 copy.22
  13.7 0.7 stack.47.info_ref
  14.8 0.7 add_convert_fusion
  15.5 0.9 slice_bitcast_fusion.1
  16.4 29.8 %all-to-all-done.received_ref = f32[32,152,128]{2,1,0:T(8,128)S(1)} async-done(((f32[32,152,128]{2,1,0:T(8,128)}), f32[32,152,128]{2,1,0:T(8,128)S(1)}, u32[]{:S(2)}, u32[]{:S(2)}) %all-to-all-start) | async-done | bytes 2490400 | tf_op jit(solution)/shard_map/all_to_all | solution.py:340
  46.4 0.3 collective-permute-start
  46.7 1.1 pad_maximum_fusion.adj_any
  47.7 1.7 %stage_first_pair.1 = (bf16[2,32,72,256]{3,2,1,0:T(8,128)(2,1)S(1)}, bf16[2,512,512]{2,1,0:T(8,128)(2,1)S(1)}, bf16[2,512,256]{2,1,0:T(8,128)(2,1)S(1)}) custom-call(f32[32,152,128]{2,1,0:T(8,128)S(1)} %all-to-all-done.received_ref, bf16[8,32,72,256]{3,2,1,0:T(8,128)(2,1)} %dual_hbm.3, bf16[2,512,512]{2,1,0:T(8,128)(2,1)S(1)} %maximum_maximum_fusion.fwd_any, ...), custom_call_target="tpu_custom_call" | custom-call | tf_op jit(solution)/shard_map/stage_first_pair/pallas_call | solution.py:352
  49.4 1.3 %collective-permute-done.edge_ref = f32[32,4,128]{2,1,0:T(4,128)S(1)} collective-permute-done((f32[32,4,128]{2,1,0:T(4,128)S(1)}, f32[32,4,128]{2,1,0:T(4,128)S(1)}, u32[]{:S(2)}, u32[]{:S(2)}) %collective-permute-start) | collective-permute-done | bytes 65568 | tf_op jit(solution)/shard_map/ppermute | solution.py:22
  50.7 15.1 %facet_update.1 = (bf16[8,32,72,256]{3,2,1,0:T(8,128)(2,1)}, bf16[2,32,72,256]{3,2,1,0:T(8,128)(2,1)S(1)}, f32[32,152,128]{2,1,0:T(8,128)S(1)}, f32[32,4,128]{2,1,0:T(4,128)S(1)}, f32[32,152,128]{2,1,0:T(8,128)S(1)}) custom-call(f32[16]{0:T(128)S(1)} %reshape.70.taps_ref, f32[8]{0:T(128)S(1)} %copy-done.1, ...), custom_call_target="tpu_custom_call", output_to_operand_aliasing={{4}: (4, {})} | custom-call | tf_op jit(solution)/shard_map/facet_update/pallas_call | solution.py:372
  65.8 0.8 collective-permute-start.1
  66.6 1.4 %store_last_pair.1 = (bf16[8,32,72,256]{3,2,1,0:T(8,128)(2,1)}, f32[8,128]{1,0:T(8,128)S(1)}) custom-call(bf16[2,32,72,256]{3,2,1,0:T(8,128)(2,1)S(1)} %get-tuple-element.14.tail_ref, bf16[8,32,72,256]{3,2,1,0:T(8,128)(2,1)} %get-tuple-element.15.begun_hbm), custom_call_target="tpu_custom_call", output_to_operand_aliasing={{0}: (1, {})} | custom-call | tf_op jit(solution)/shard_map/store_last_pair/pallas_call | solution.py:398
  68.0 3.3 %collective-permute-done.1.spill_ref = f32[32,4,128]{2,1,0:T(4,128)S(1)} collective-permute-done((f32[32,4,128]{2,1,0:T(4,128)S(1)}, f32[32,4,128]{2,1,0:T(4,128)S(1)}, u32[]{:S(2)}, u32[]{:S(2)}) %collective-permute-start.1) | collective-permute-done | bytes 65568 | tf_op jit(solution)/shard_map/ppermute | solution.py:22
  71.3 0.6 add_border_rows.1
  71.9 35.8 %all_to_all.10.block_ref = f32[32,152,128]{2,1,0:T(8,128)S(1)} all-to-all(f32[32,152,128]{2,1,0:T(8,128)S(1)} %add_border_rows.1), channel_id=1, replica_groups=mesh['grp'=4,'fac'=32] {'fac'}, dimensions={0} | all-to-all | bytes 4980736 | tf_op jit(solution)/shard_map/all_to_all | solution.py:417
  107.7 2.1 %unpack_facets.1 = f32[1,1536,256]{2,1,0:T(8,128)} custom-call(s32[4,32]{1,0:T(4,128)S(1)} %copy-done, f32[32,152,128]{2,1,0:T(8,128)S(1)} %all_to_all.10.block_ref), custom_call_target="tpu_custom_call" | custom-call | tf_op jit(solution)/shard_map/unpack_facets/pallas_call | solution.py:419
  (23 shorter events, 0.6 us)
Async XLA Ops:
  3.5 8.2 %copy-start = (s32[4,32]{1,0:T(4,128)S(1)}, s32[4,32]{1,0:T(4,128)}, u32[]{:S(2)}) copy-start(s32[4,32]{1,0:T(4,128)} %rows_ref.1) | copy-start | bytes 1540
  3.5 9.5 %copy-start.2 = (bf16[2,4]{1,0:T(2,128)(2,1)S(1)}, bf16[2,4]{1,0:T(2,128)(2,1)}, u32[]{:S(2)}) copy-start(bf16[2,4]{1,0:T(2,128)(2,1)} %param.7) | copy-start | bytes 52
  3.5 42.8 %all-to-all-start = ((f32[32,152,128]{2,1,0:T(8,128)}), f32[32,152,128]{2,1,0:T(8,128)S(1)}, u32[]{:S(2)}, u32[]{:S(2)}) async-start(f32[32,152,128]{2,1,0:T(8,128)} %pack_facets.1), calls=%async_computation | async-start | bytes 4980736 | tf_op jit(solution)/shard_map/all_to_all | solution.py:340
  46.4 4.3 %collective-permute-start = (f32[32,4,128]{2,1,0:T(4,128)S(1)}, f32[32,4,128]{2,1,0:T(4,128)S(1)}, u32[]{:S(2)}, u32[]{:S(2)}) collective-permute-start(f32[32,4,128]{2,1,0:T(4,128)S(1)} %pad_maximum_fusion.1), channel_id=1, source_target_pairs={{0,32},{1,97},{2,34},{3,99},{4,36},{5,101},{6,38},{7,103},{8,40},{... | collective-permute-start | bytes 196616 | tf_op jit(solution)/shard_map/ppermute | solution.py:22
  47.7 3.0 %copy-start.1 = (f32[8]{0:T(128)S(1)}, f32[8]{0:T(128)}, u32[]{:S(2)}) copy-start(f32[8]{0:T(128)} %thr_ref.1) | copy-start | bytes 100
  65.8 5.5 %collective-permute-start.1 = (f32[32,4,128]{2,1,0:T(4,128)S(1)}, f32[32,4,128]{2,1,0:T(4,128)S(1)}, u32[]{:S(2)}, u32[]{:S(2)}) collective-permute-start(f32[32,4,128]{2,1,0:T(4,128)S(1)} %get-tuple-element.18), channel_id=1, source_target_pairs={{0,96},{1,33},{2,98},{3,35},{4,100},{5,37},{6,102},{7,39},{8,104},... | collective-permute-start | bytes 196616 | tf_op jit(solution)/shard_map/ppermute | solution.py:22

commit v7 on v6

--- a/solution.py
+++ b/solution.py
@@ -126,11 +126,13 @@
             copies[-1].start()
 
     shared = lax.broadcasted_iota(jnp.int32, (8, LANES), 0) < 3
-    early = 3 * facets // 4
-    ready = (band_rows - (facets - early) * capacity) // 8 * 8 - 8
+    sent = 8
+    early = (facets // 2, 3 * facets // 4, 7 * facets // 8, 15 * facets // 16)
     for q in range(facets):
-        if q == early:
-            send(8, ready)
+        if q in early:
+            ready = (band_rows - (facets - q) * capacity) // 8 * 8 - 8
+            send(sent, ready)
+            sent = ready
         begin = starts[q] + (MARGIN - ABOVE)
         for h in range(2):
             before = strip[h, pl.ds(begin, 8)]
@@ -140,7 +142,7 @@
         strip[h, end - ABOVE : end] += strip[h, MARGIN - ABOVE : MARGIN]
         strip[h, MARGIN : MARGIN + 1] += strip[h, end : end + 1]
     send(0, 8)
-    send(ready, band_rows)
+    send(sent, band_rows)
     for copy in copies:
         copy.wait()
 
@@ -421,7 +423,7 @@
         out_shape=jax.ShapeDtypeStruct(image_cube.shape, jnp.float32),
         in_specs=[smem, vmem],
         out_specs=hbm,
-        scratch_shapes=row_scratch[:2] + [pltpu.SemaphoreType.DMA((6,))],
+        scratch_shapes=row_scratch[:2] + [pltpu.SemaphoreType.DMA((12,))],
         compiler_params=pltpu.CompilerParams(vmem_limit_bytes=16 << 20),
         name="unpack_facets",
     )(facet_rows, returned)

time: 111 us -> 111 us (level)
  no operation moved by 1% of the time
where the time goes in v7:
time: 111 us; the launch traced here: 110 us
  blocking collectives  35.8 us (32%)
  waiting for transfers between devices  34.4 us (31%)
  Pallas kernels  23.8 us (21%)
  starting transfers between devices  9.28 us (8%)
  local copies, waits for them, and re-layouts  2.81 us (3%)
  other arithmetic  2.3 us (2%)
  between operations  1.5 us (1%)
    all_to_all x1, blocking collectives, on_device(): lax.all_to_all(merged, 'fac', split_axis=0, concat_axis=0, tiled=True)  35.8 us
    all_to_all x1, waiting for transfers between devices, on_device(): lax.all_to_all(packed, 'fac', split_axis=0, concat_axis=0, tiled=True)  29.8 us
    pallas_call x1, Pallas kernels, on_device(): pl.pallas_call(functools.partial(facet_kernel, group, ext), out_shape=(pl...  15.1 us
    all_to_all x1, starting transfers between devices, on_device(): lax.all_to_all(packed, 'fac', split_axis=0, concat_axis=0, tiled=True)  8.18 us
    ppermute x2, waiting for transfers between devices, border_shift(): return lax.ppermute(x, ('grp', 'fac'), pairs)  4.57 us
    pallas_call x1, Pallas kernels, on_device(): pl.pallas_call(functools.partial(pack_kernel, per_step, ext), out_shape=p...  2.85 us
  transfers between devices with their start and end apart: 3, of which 3 were waited for; matrix products, arithmetic and copies ran while one was open for 5% of the time, Pallas kernels for 3%

profile of v7, /device:TPU:24, one launch (start us, length us, event | category | flops | bytes accessed | tf_op | source)
XLA Modules:
  0.0 109.8 jit_solution(7756047045078891462)
XLA Ops:
  0.6 2.8 %pack_facets.1 = f32[32,152,128]{2,1,0:T(8,128)} custom-call(s32[4,32]{1,0:T(4,128)} %rows_ref.1, f32[1,1536,256]{2,1,0:T(8,128)} %image_ref.1), custom_call_target="tpu_custom_call" | custom-call | tf_op jit(solution)/shard_map/pack_facets/pallas_call | solution.py:327
  3.5 8.2 %all-to-all-start = ((f32[32,152,128]{2,1,0:T(8,128)}), f32[32,152,128]{2,1,0:T(8,128)S(1)}, u32[]{:S(2)}, u32[]{:S(2)}) async-start(f32[32,152,128]{2,1,0:T(8,128)} %pack_facets.1), calls=%async_computation | async-start | bytes 4980736 | tf_op jit(solution)/shard_map/all_to_all | solution.py:342
  11.7 0.6 dynamic_slice.13
  13.0 0.1 rev.3
  13.1 0.1 reshape.70.taps_ref
  13.3 0.1 copy.19
  13.4 0.1 copy.20
  13.5 0.1 copy.21
  13.6 0.1 copy.22
  13.7 0.7 stack.47.info_ref
  14.8 0.7 add_convert_fusion
  15.5 0.9 slice_bitcast_fusion.1
  16.4 29.8 %all-to-all-done.received_ref = f32[32,152,128]{2,1,0:T(8,128)S(1)} async-done(((f32[32,152,128]{2,1,0:T(8,128)}), f32[32,152,128]{2,1,0:T(8,128)S(1)}, u32[]{:S(2)}, u32[]{:S(2)}) %all-to-all-start) | async-done | bytes 2490400 | tf_op jit(solution)/shard_map/all_to_all | solution.py:342
  46.4 0.3 collective-permute-start
  46.7 1.1 pad_maximum_fusion.adj_any
  47.7 1.7 %stage_first_pair.1 = (bf16[2,32,72,256]{3,2,1,0:T(8,128)(2,1)S(1)}, bf16[2,512,512]{2,1,0:T(8,128)(2,1)S(1)}, bf16[2,512,256]{2,1,0:T(8,128)(2,1)S(1)}) custom-call(f32[32,152,128]{2,1,0:T(8,128)S(1)} %all-to-all-done.received_ref, bf16[8,32,72,256]{3,2,1,0:T(8,128)(2,1)} %dual_hbm.3, bf16[2,512,512]{2,1,0:T(8,128)(2,1)S(1)} %maximum_maximum_fusion.fwd_any, ...), custom_call_target="tpu_custom_call" | custom-call | tf_op jit(solution)/shard_map/stage_first_pair/pallas_call | solution.py:354
  49.4 1.3 %collective-permute-done.edge_ref = f32[32,4,128]{2,1,0:T(4,128)S(1)} collective-permute-done((f32[32,4,128]{2,1,0:T(4,128)S(1)}, f32[32,4,128]{2,1,0:T(4,128)S(1)}, u32[]{:S(2)}, u32[]{:S(2)}) %collective-permute-start) | collective-permute-done | bytes 65568 | tf_op jit(solution)/shard_map/ppermute | solution.py:22
  50.7 15.1 %facet_update.1 = (bf16[8,32,72,256]{3,2,1,0:T(8,128)(2,1)}, bf16[2,32,72,256]{3,2,1,0:T(8,128)(2,1)S(1)}, f32[32,152,128]{2,1,0:T(8,128)S(1)}, f32[32,4,128]{2,1,0:T(4,128)S(1)}, f32[32,152,128]{2,1,0:T(8,128)S(1)}) custom-call(f32[16]{0:T(128)S(1)} %reshape.70.taps_ref, f32[8]{0:T(128)S(1)} %copy-done.1, ...), custom_call_target="tpu_custom_call", output_to_operand_aliasing={{4}: (4, {})} | custom-call | tf_op jit(solution)/shard_map/facet_update/pallas_call | solution.py:374
  65.8 0.8 collective-permute-start.1
  66.6 1.4 %store_last_pair.1 = (bf16[8,32,72,256]{3,2,1,0:T(8,128)(2,1)}, f32[8,128]{1,0:T(8,128)S(1)}) custom-call(bf16[2,32,72,256]{3,2,1,0:T(8,128)(2,1)S(1)} %get-tuple-element.14.tail_ref, bf16[8,32,72,256]{3,2,1,0:T(8,128)(2,1)} %get-tuple-element.15.begun_hbm), custom_call_target="tpu_custom_call", output_to_operand_aliasing={{0}: (1, {})} | custom-call | tf_op jit(solution)/shard_map/store_last_pair/pallas_call | solution.py:400
  68.0 3.3 %collective-permute-done.1.spill_ref = f32[32,4,128]{2,1,0:T(4,128)S(1)} collective-permute-done((f32[32,4,128]{2,1,0:T(4,128)S(1)}, f32[32,4,128]{2,1,0:T(4,128)S(1)}, u32[]{:S(2)}, u32[]{:S(2)}) %collective-permute-start.1) | collective-permute-done | bytes 65568 | tf_op jit(solution)/shard_map/ppermute | solution.py:22
  71.3 0.6 add_border_rows.1
  71.9 35.8 %all_to_all.10.block_ref = f32[32,152,128]{2,1,0:T(8,128)S(1)} all-to-all(f32[32,152,128]{2,1,0:T(8,128)S(1)} %add_border_rows.1), channel_id=1, replica_groups=mesh['grp'=4,'fac'=32] {'fac'}, dimensions={0} | all-to-all | bytes 4980736 | tf_op jit(solution)/shard_map/all_to_all | solution.py:419
  107.7 2.1 %unpack_facets.1 = f32[1,1536,256]{2,1,0:T(8,128)} custom-call(s32[4,32]{1,0:T(4,128)S(1)} %copy-done, f32[32,152,128]{2,1,0:T(8,128)S(1)} %all_to_all.10.block_ref), custom_call_target="tpu_custom_call" | custom-call | tf_op jit(solution)/shard_map/unpack_facets/pallas_call | solution.py:421
  (23 shorter events, 0.6 us)
Async XLA Ops:
  3.5 8.2 %copy-start = (s32[4,32]{1,0:T(4,128)S(1)}, s32[4,32]{1,0:T(4,128)}, u32[]{:S(2)}) copy-start(s32[4,32]{1,0:T(4,128)} %rows_ref.1) | copy-start | bytes 1540
  3.5 9.5 %copy-start.2 = (bf16[2,4]{1,0:T(2,128)(2,1)S(1)}, bf16[2,4]{1,0:T(2,128)(2,1)}, u32[]{:S(2)}) copy-start(bf16[2,4]{1,0:T(2,128)(2,1)} %param.7) | copy-start | bytes 52
  3.5 42.8 %all-to-all-start = ((f32[32,152,128]{2,1,0:T(8,128)}), f32[32,152,128]{2,1,0:T(8,128)S(1)}, u32[]{:S(2)}, u32[]{:S(2)}) async-start(f32[32,152,128]{2,1,0:T(8,128)} %pack_facets.1), calls=%async_computation | async-start | bytes 4980736 | tf_op jit(solution)/shard_map/all_to_all | solution.py:342
  46.4 4.3 %collective-permute-start = (f32[32,4,128]{2,1,0:T(4,128)S(1)}, f32[32,4,128]{2,1,0:T(4,128)S(1)}, u32[]{:S(2)}, u32[]{:S(2)}) collective-permute-start(f32[32,4,128]{2,1,0:T(4,128)S(1)} %pad_maximum_fusion.1), channel_id=1, source_target_pairs={{0,32},{1,97},{2,34},{3,99},{4,36},{5,101},{6,38},{7,103},{8,40},{... | collective-permute-start | bytes 196616 | tf_op jit(solution)/shard_map/ppermute | solution.py:22
  47.7 3.0 %copy-start.1 = (f32[8]{0:T(128)S(1)}, f32[8]{0:T(128)}, u32[]{:S(2)}) copy-start(f32[8]{0:T(128)} %thr_ref.1) | copy-start | bytes 100
  65.8 5.5 %collective-permute-start.1 = (f32[32,4,128]{2,1,0:T(4,128)S(1)}, f32[32,4,128]{2,1,0:T(4,128)S(1)}, u32[]{:S(2)}, u32[]{:S(2)}) collective-permute-start(f32[32,4,128]{2,1,0:T(4,128)S(1)} %get-tuple-element.18), channel_id=1, source_target_pairs={{0,96},{1,33},{2,98},{3,35},{4,100},{5,37},{6,102},{7,39},{8,104},... | collective-permute-start | bytes 196616 | tf_op jit(solution)/shard_map/ppermute | solution.py:22

commit v8 on v7

--- a/solution.py
+++ b/solution.py
@@ -257,10 +257,7 @@
             if stage < steps:
                 analyse(stage, i)
 
-        if stage > 0:
-            pl.loop(0, channels // group)(lambda i: synthesise(stage - 1, i))
-        if stage < steps:
-            pl.loop(0, channels // group)(lambda i: analyse(stage, i))
+        pl.loop(0, channels // group)(work)
         if stage == 1:
             fetches[3].start()
         if 0 < stage < steps:

time: 111 us -> 111 us (level)
  no operation moved by 1% of the time
where the time goes in v8:
time: 111 us; the launch traced here: 110 us
  blocking collectives  35.8 us (32%)
  waiting for transfers between devices  34.4 us (31%)
  Pallas kernels  23.7 us (21%)
  starting transfers between devices  9.28 us (8%)
  local copies, waits for them, and re-layouts  2.81 us (3%)
  other arithmetic  2.3 us (2%)
  between operations  1.5 us (1%)
    all_to_all x1, blocking collectives, on_device(): lax.all_to_all(merged, 'fac', split_axis=0, concat_axis=0, tiled=True)  35.8 us
    all_to_all x1, waiting for transfers between devices, on_device(): lax.all_to_all(packed, 'fac', split_axis=0, concat_axis=0, tiled=True)  29.8 us
    pallas_call x1, Pallas kernels, on_device(): pl.pallas_call(functools.partial(facet_kernel, group, ext), out_shape=(pl...  15 us
    all_to_all x1, starting transfers between devices, on_device(): lax.all_to_all(packed, 'fac', split_axis=0, concat_axis=0, tiled=True)  8.18 us
    ppermute x2, waiting for transfers between devices, border_shift(): return lax.ppermute(x, ('grp', 'fac'), pairs)  4.57 us
    pallas_call x1, Pallas kernels, on_device(): pl.pallas_call(functools.partial(pack_kernel, per_step, ext), out_shape=p...  2.85 us
  transfers between devices with their start and end apart: 3, of which 3 were waited for; matrix products, arithmetic and copies ran while one was open for 5% of the time, Pallas kernels for 3%

profile of v8, /device:TPU:24, one launch (start us, length us, event | category | flops | bytes accessed | tf_op | source)
XLA Modules:
  0.0 109.8 jit_solution(8441284349408756270)
XLA Ops:
  0.6 2.8 %pack_facets.1 = f32[32,152,128]{2,1,0:T(8,128)} custom-call(s32[4,32]{1,0:T(4,128)} %rows_ref.1, f32[1,1536,256]{2,1,0:T(8,128)} %image_ref.1), custom_call_target="tpu_custom_call" | custom-call | tf_op jit(solution)/shard_map/pack_facets/pallas_call | solution.py:324
  3.5 8.2 %all-to-all-start = ((f32[32,152,128]{2,1,0:T(8,128)}), f32[32,152,128]{2,1,0:T(8,128)S(1)}, u32[]{:S(2)}, u32[]{:S(2)}) async-start(f32[32,152,128]{2,1,0:T(8,128)} %pack_facets.1), calls=%async_computation | async-start | bytes 4980736 | tf_op jit(solution)/shard_map/all_to_all | solution.py:339
  11.7 0.6 dynamic_slice.13
  13.0 0.1 rev.3
  13.1 0.1 reshape.70.taps_ref
  13.3 0.1 copy.19
  13.4 0.1 copy.20
  13.5 0.1 copy.21
  13.6 0.1 copy.22
  13.7 0.7 stack.47.info_ref
  14.8 0.7 add_convert_fusion
  15.5 0.9 slice_bitcast_fusion.1
  16.4 29.8 %all-to-all-done.received_ref = f32[32,152,128]{2,1,0:T(8,128)S(1)} async-done(((f32[32,152,128]{2,1,0:T(8,128)}), f32[32,152,128]{2,1,0:T(8,128)S(1)}, u32[]{:S(2)}, u32[]{:S(2)}) %all-to-all-start) | async-done | bytes 2490400 | tf_op jit(solution)/shard_map/all_to_all | solution.py:339
  46.4 0.3 collective-permute-start
  46.7 1.1 pad_maximum_fusion.adj_any
  47.7 1.7 %stage_first_pair.1 = (bf16[2,32,72,256]{3,2,1,0:T(8,128)(2,1)S(1)}, bf16[2,512,512]{2,1,0:T(8,128)(2,1)S(1)}, bf16[2,512,256]{2,1,0:T(8,128)(2,1)S(1)}) custom-call(f32[32,152,128]{2,1,0:T(8,128)S(1)} %all-to-all-done.received_ref, bf16[8,32,72,256]{3,2,1,0:T(8,128)(2,1)} %dual_hbm.3, bf16[2,512,512]{2,1,0:T(8,128)(2,1)S(1)} %maximum_maximum_fusion.fwd_any, ...), custom_call_target="tpu_custom_call" | custom-call | tf_op jit(solution)/shard_map/stage_first_pair/pallas_call | solution.py:351
  49.4 1.3 %collective-permute-done.edge_ref = f32[32,4,128]{2,1,0:T(4,128)S(1)} collective-permute-done((f32[32,4,128]{2,1,0:T(4,128)S(1)}, f32[32,4,128]{2,1,0:T(4,128)S(1)}, u32[]{:S(2)}, u32[]{:S(2)}) %collective-permute-start) | collective-permute-done | bytes 65568 | tf_op jit(solution)/shard_map/ppermute | solution.py:22
  50.7 15.0 %facet_update.1 = (bf16[8,32,72,256]{3,2,1,0:T(8,128)(2,1)}, bf16[2,32,72,256]{3,2,1,0:T(8,128)(2,1)S(1)}, f32[32,152,128]{2,1,0:T(8,128)S(1)}, f32[32,4,128]{2,1,0:T(4,128)S(1)}, f32[32,152,128]{2,1,0:T(8,128)S(1)}) custom-call(f32[16]{0:T(128)S(1)} %reshape.70.taps_ref, f32[8]{0:T(128)S(1)} %copy-done.1, ...), custom_call_target="tpu_custom_call", output_to_operand_aliasing={{4}: (4, {})} | custom-call | tf_op jit(solution)/shard_map/facet_update/pallas_call | solution.py:371
  65.7 0.8 collective-permute-start.1
  66.5 1.4 %store_last_pair.1 = (bf16[8,32,72,256]{3,2,1,0:T(8,128)(2,1)}, f32[8,128]{1,0:T(8,128)S(1)}) custom-call(bf16[2,32,72,256]{3,2,1,0:T(8,128)(2,1)S(1)} %get-tuple-element.14.tail_ref, bf16[8,32,72,256]{3,2,1,0:T(8,128)(2,1)} %get-tuple-element.15.begun_hbm), custom_call_target="tpu_custom_call", output_to_operand_aliasing={{0}: (1, {})} | custom-call | tf_op jit(solution)/shard_map/store_last_pair/pallas_call | solution.py:397
  68.0 3.3 %collective-permute-done.1.spill_ref = f32[32,4,128]{2,1,0:T(4,128)S(1)} collective-permute-done((f32[32,4,128]{2,1,0:T(4,128)S(1)}, f32[32,4,128]{2,1,0:T(4,128)S(1)}, u32[]{:S(2)}, u32[]{:S(2)}) %collective-permute-start.1) | collective-permute-done | bytes 65568 | tf_op jit(solution)/shard_map/ppermute | solution.py:22
  71.3 0.6 add_border_rows.1
  71.8 35.8 %all_to_all.10.block_ref = f32[32,152,128]{2,1,0:T(8,128)S(1)} all-to-all(f32[32,152,128]{2,1,0:T(8,128)S(1)} %add_border_rows.1), channel_id=1, replica_groups=mesh['grp'=4,'fac'=32] {'fac'}, dimensions={0} | all-to-all | bytes 4980736 | tf_op jit(solution)/shard_map/all_to_all | solution.py:416
  107.6 2.1 %unpack_facets.1 = f32[1,1536,256]{2,1,0:T(8,128)} custom-call(s32[4,32]{1,0:T(4,128)S(1)} %copy-done, f32[32,152,128]{2,1,0:T(8,128)S(1)} %all_to_all.10.block_ref), custom_call_target="tpu_custom_call" | custom-call | tf_op jit(solution)/shard_map/unpack_facets/pallas_call | solution.py:418
  (23 shorter events, 0.6 us)
Async XLA Ops:
  3.5 8.2 %copy-start = (s32[4,32]{1,0:T(4,128)S(1)}, s32[4,32]{1,0:T(4,128)}, u32[]{:S(2)}) copy-start(s32[4,32]{1,0:T(4,128)} %rows_ref.1) | copy-start | bytes 1540
  3.5 9.5 %copy-start.2 = (bf16[2,4]{1,0:T(2,128)(2,1)S(1)}, bf16[2,4]{1,0:T(2,128)(2,1)}, u32[]{:S(2)}) copy-start(bf16[2,4]{1,0:T(2,128)(2,1)} %param.7) | copy-start | bytes 52
  3.5 42.8 %all-to-all-start = ((f32[32,152,128]{2,1,0:T(8,128)}), f32[32,152,128]{2,1,0:T(8,128)S(1)}, u32[]{:S(2)}, u32[]{:S(2)}) async-start(f32[32,152,128]{2,1,0:T(8,128)} %pack_facets.1), calls=%async_computation | async-start | bytes 4980736 | tf_op jit(solution)/shard_map/all_to_all | solution.py:339
  46.4 4.3 %collective-permute-start = (f32[32,4,128]{2,1,0:T(4,128)S(1)}, f32[32,4,128]{2,1,0:T(4,128)S(1)}, u32[]{:S(2)}, u32[]{:S(2)}) collective-permute-start(f32[32,4,128]{2,1,0:T(4,128)S(1)} %pad_maximum_fusion.1), channel_id=1, source_target_pairs={{0,32},{1,97},{2,34},{3,99},{4,36},{5,101},{6,38},{7,103},{8,40},{... | collective-permute-start | bytes 196616 | tf_op jit(solution)/shard_map/ppermute | solution.py:22
  47.7 3.0 %copy-start.1 = (f32[8]{0:T(128)S(1)}, f32[8]{0:T(128)}, u32[]{:S(2)}) copy-start(f32[8]{0:T(128)} %thr_ref.1) | copy-start | bytes 100
  65.7 5.5 %collective-permute-start.1 = (f32[32,4,128]{2,1,0:T(4,128)S(1)}, f32[32,4,128]{2,1,0:T(4,128)S(1)}, u32[]{:S(2)}, u32[]{:S(2)}) collective-permute-start(f32[32,4,128]{2,1,0:T(4,128)S(1)} %get-tuple-element.18), channel_id=1, source_target_pairs={{0,96},{1,33},{2,98},{3,35},{4,100},{5,37},{6,102},{7,39},{8,104},... | collective-permute-start | bytes 196616 | tf_op jit(solution)/shard_map/ppermute | solution.py:22
